TPU v7x, 512 devices: a whole 4x4x16 slice. The times are simulated.
512 devices in a mesh: node: 32 (over z, x_lo), local: 16 (over y, x_hi, core).
Axes of the slice: x: 4 (x_hi: 2, x_lo: 2; x = x_hi * 2 + x_lo), y: 4, z: 16, core: 2. Of those that a mesh axis runs over, the one named last changes fastest.
Arguments:
- tokens: bfloat16 [131072, 4096], P(('node', 'local')), may hold values from -6 to 6
- gain: float32 [4096], replicated, may hold values from 0.1 to 1.9
- w_codes: bfloat16 [4, 4096, 128], P(None, ('node', 'local')), may hold values from -1 to 1
- w_scales: bfloat16 [4, 4096], P(None, ('node', 'local')), may hold values from 0.0099487305 to 0.049804688
- seq_counts: int32 [512], P(('node', 'local')), may hold values from 1 to 4, as said below
- key_grad: bfloat16 [131072, 512], P(('node', 'local')), may hold values from -6 to 6
Outputs:
- keys: bfloat16 [131072, 512], P(('node', 'local'))
- token_input_grad: bfloat16 [131072, 4096], P(('node', 'local'))
- weight_grad: float32 [4096, 512], P(('node', 'local'))
- gain_grad: float32 [4096], replicated
Inputs may be any that keep to these rules, and one draw needn't show every extreme that they name: `seq_counts`: some device has exactly 4 live sequences.
All inputs are finite; a program needn't handle non-finite values. Where the computation divides by a largest or mean magnitude, that divisor is 1e-20 or more.
Results may differ from a plain program's by a relative error of at most 0.012.
Values may be sent and summed in bfloat16 or wider, within the bound.
A program may use at most 192 MiB of HBM per device.

v0:
```python
import math

import jax
import jax.numpy as jnp
from jax import lax
from jax.sharding import PartitionSpec as P

BLOCK = 128
SEQ_LEN = 64


def build_weight(codes, scales):
    pieces = [
        (codes[c].astype(jnp.float32) * scales[c].astype(jnp.float32)[:, None]).astype(jnp.bfloat16)
        for c in range(codes.shape[0])
    ]
    return jnp.concatenate(pieces, axis=1)


def quantize_blocks(part, blocks_count):
    code_list = []
    scale_list = []
    for c in range(blocks_count):
        block_part = part[:, c * BLOCK : (c + 1) * BLOCK]
        scale_row = (jnp.max(jnp.abs(block_part), axis=1) + 1e-06).astype(jnp.bfloat16)
        code_list.append((block_part / scale_row.astype(jnp.float32)[:, None]).astype(jnp.bfloat16))
        scale_list.append(scale_row)
    return (jnp.stack(code_list, axis=0), jnp.stack(scale_list, axis=0))


def expand_codes(codes, scales):
    widened = jnp.repeat(scales.astype(jnp.float32), BLOCK, axis=-1)
    return codes.astype(jnp.float32) * widened


def local(tokens, gain, w_codes, w_scales, seq_counts, key_grad):
    rows = tokens.shape[0]
    node_count = lax.axis_size("node")
    local_count = lax.axis_size("local")
    inverse = 1.0 / math.sqrt(rows * node_count * local_count)
    full_codes, full_scales = (
        lax.all_gather(w_codes, ("node", "local"), axis=1, tiled=True),
        lax.all_gather(w_scales, ("node", "local"), axis=1, tiled=True),
    )
    weight = build_weight(full_codes, full_scales)
    blocks_count, depth, block_width = full_codes.shape
    kv_width = blocks_count * block_width
    shard_rows = depth // (node_count * local_count)
    slots = lax.broadcasted_iota(jnp.int32, (rows, 1), 0) // SEQ_LEN
    live = slots < seq_counts[0]
    input_float = tokens.astype(jnp.float32)
    inverse_root_mean = lax.rsqrt(
        jnp.mean(input_float * input_float, axis=-1, keepdims=True) + 1e-05
    )
    input_normalized = input_float * inverse_root_mean
    normalized_rows = (input_normalized * gain).astype(jnp.bfloat16)
    keys = jnp.where(
        live, jnp.dot(normalized_rows, weight, preferred_element_type=jnp.float32), 0.0
    ).astype(jnp.bfloat16)
    masked = jnp.where(live, key_grad, jnp.zeros_like(key_grad))
    slab = depth // local_count
    begin = lax.axis_index("local") * slab
    kept_codes = lax.dynamic_slice_in_dim(full_codes, begin, slab, 1)
    kept_scales = lax.dynamic_slice_in_dim(full_scales, begin, slab, 1)
    back_codes, back_scales = (
        lax.all_gather(kept_codes, "local", axis=1, tiled=True),
        lax.all_gather(kept_scales, "local", axis=1, tiled=True),
    )
    back_weight = build_weight(back_codes, back_scales)
    normalized_grad = lax.dot_general(
        masked, back_weight, (((1,), (1,)), ((), ())), preferred_element_type=jnp.float32
    )
    scaled_grad = normalized_grad * gain
    token_input_grad = (
        inverse_root_mean
        * (
            scaled_grad
            - input_normalized * jnp.mean(scaled_grad * input_normalized, axis=-1, keepdims=True)
        )
    ).astype(jnp.bfloat16)
    gain_grad_total = lax.psum(
        jnp.sum(normalized_grad * input_normalized, axis=0), ("node", "local")
    )
    part = lax.dot_general(
        normalized_rows, masked, (((0,), (0,)), ((), ())), preferred_element_type=jnp.float32
    )
    codes, scales = quantize_blocks(part, blocks_count)
    group_rows = local_count * shard_rows
    codes_flat = codes.reshape(blocks_count, node_count, group_rows * block_width)
    scales_flat = scales.reshape(blocks_count, node_count, group_rows)
    got_codes, got_scales = (
        lax.all_to_all(codes_flat, "local", split_axis=2, concat_axis=0, tiled=True),
        lax.all_to_all(scales_flat, "local", split_axis=2, concat_axis=0, tiled=True),
    )
    restored = expand_codes(
        got_codes.reshape(local_count, blocks_count, node_count, shard_rows * block_width),
        got_scales.reshape(local_count, blocks_count, node_count, shard_rows),
    )
    group_sum = jnp.sum(restored, axis=0)
    arrived = lax.all_to_all(group_sum, "node", split_axis=1, concat_axis=0, tiled=True)
    final = jnp.sum(arrived.reshape(node_count, blocks_count, shard_rows * block_width), axis=0)
    weight_grad = (
        final.reshape(blocks_count, shard_rows, block_width)
        .transpose(1, 0, 2)
        .reshape(shard_rows, kv_width)
        * inverse
    )
    return (keys, token_input_grad, weight_grad, gain_grad_total * inverse)


def solution(mesh):
    return jax.shard_map(
        local,
        mesh=mesh,
        in_specs=(
            P(("node", "local"), None),
            P(),
            P(None, ("node", "local"), None),
            P(None, ("node", "local")),
            P(("node", "local")),
            P(("node", "local"), None),
        ),
        out_specs=(
            P(("node", "local"), None),
            P(("node", "local"), None),
            P(("node", "local"), None),
            P(),
        ),
        check_vma=False,
    )
```

profile of v0, /device:TPU:1, one launch (start us, length us, event | category | flops | bytes accessed | tf_op | source)
XLA Modules:
  0.0 1732.1 jit_solution(4162968902317516966)
XLA Ops:
  7.2 0.0 all-gather.4.cloned.1.call-start
  7.2 0.7 all-gather.4.cloned.1.call-update
  8.6 2.1 fusion.12
  10.7 3.1 fusion.43
  13.7 0.0 copy-start
  13.7 0.6 abs_reduce_fusion.3
  14.3 2.6 copy-done
  17.0 0.1 copy.38
  17.1 0.8 reshape.276
  17.9 10.2 all-to-all-start.1
  28.1 5.5 divide_convert_fusion.3
  33.5 2.3 copy.33
  35.8 2.3 stack.22
  38.1 1.3 copy.34
  39.4 2.3 stack.23
  41.7 0.7 copy.35
  42.4 1.3 stack.24
  43.7 0.0 copy-start.2
  43.7 0.7 copy.36
  44.3 0.5 stack.25
  44.8 0.1 copy-done.2
  44.9 3.4 pad_maximum_fusion
  48.3 20.2 %copy.37 = bf16[4,32,16384]{1,0,2:T(4,128)(2,1)} copy(bf16[4,32,16384]{2,1,0:T(8,128)(2,1)} %pad_maximum_fusion) | data formatting | bytes 8388608 | tf_op jit(solution)/shard_map/stack | solution.py:28
  68.5 20.8 %reshape.278 = bf16[16,2,65536]{2,1,0:T(2,128)(2,1)} reshape(bf16[16384,4,32]{2,1,0:T(4,128)(2,1)} %bitcast.96) | data formatting | bytes 8388608
  89.3 0.0 all-to-all-done.1
  89.3 7.3 all-to-all-start
  96.5 0.0 all-gather.6.cloned.1.call-start
  96.6 731.4 %all-gather.4.cloned.1.call-done = bf16[4,4096,128]{2,1,0:T(8,128)(2,1)} async-done(((bf16[4,8,128]{2,1,0:T(8,128)(2,1)}), bf16[4,4096,128]{2,1,0:T(8,128)(2,1)}) %all-gather.4.cloned.1.call-update) | async-done | bytes 4194320 | tf_op jit(solution)/shard_map/all_gather | solution.py:42
  828.0 1.7 constant_dynamic-slice_fusion
  829.7 0.0 all-gather.6.cloned.1.call-update
  829.7 0.1 reshape.277
  829.9 0.2 copy.40
  830.1 0.0 all-to-all-done
  830.1 16.0 reshape.279
  846.1 11.0 broadcast_in_dim.27
  857.1 0.0 copy-start.5
  857.1 17.4 %fusion.1 = f32[4,32,1024]{1,0,2:T(4,128)S(1)} fusion(f32[16,4,32,1024]{2,1,3,0:T(4,128)} %bitcast.94, bf16[4,32,16,1024]{1,0,3,2:T(4,128)(2,1)} %bitcast.95), kind=kLoop, calls=%fused_computation.2 | loop fusion | flops 6160384 | bytes 13107200 | tf_op jit(solution)/shard_map/reduce_sum | solution.py:99
  874.5 1.5 copy.41
  876.0 7.5 all-to-all-start.2
  883.6 0.0 copy-done.5
  883.6 694.1 %all-gather = bf16[512,8,4]{1,2,0:T(4,128)(2,1)S(1)} all-gather(bf16[1,8,4]{1,2,0:T(4,128)(2,1)S(1)} %bitcast.109), channel_id=1, replica_groups=mesh['node'=32,'local'=16] {'node','local'}, dimensions={0}, use_global_device_ids=true | all-gather | bytes 32832 | tf_op jit(solution)/shard_map/all_gather | solution.py:43
  1577.7 0.1 copy.32
  1577.7 0.6 reshape.275
  1578.3 19.4 %all_gather.15 = bf16[4,4096]{1,0:T(4,128)(2,1)S(1)} all-gather(bf16[4,256]{1,0:T(4,128)(2,1)S(1)} %dynamic-slice_bitcast_fusion), channel_id=1, replica_groups=mesh['node'=32,'local'=16] {'local'}, dimensions={1}, use_global_device_ids=true | all-gather | bytes 34816 | tf_op jit(solution)/shard_map/all_gather | solution.py:67
  1597.8 0.0 all-to-all-done.2
  1597.8 0.1 reduce_sum.48
  1598.0 0.6 copy.45
  1598.6 0.0 copy-start.1
  1598.6 0.0 copy-start.4
  1598.6 5.7 fusion.36
  1604.3 0.0 copy-done.1
  1604.3 0.0 copy-done.4
  1604.3 2.0 fusion.40
  1606.3 0.0 all-gather.6.cloned.1.call-done
  1606.3 0.0 copy-start.3
  1606.3 5.6 fusion.32
  1611.9 0.0 copy-done.3
  1612.0 3.2 fusion.11
  1615.1 104.9 %psum.7 = f32[4096]{0:T(1024)S(1)} all-reduce(f32[4096]{0:T(1024)S(1)} %get-tuple-element.8), channel_id=1, replica_groups=mesh['node'=32,'local'=16] {'node','local'}, use_global_device_ids=true, to_apply=%region_9.10 | all-reduce | flops 4096 | bytes 32768 | tf_op jit(solution)/shard_map/psum | solution.py:81
  1720.0 0.6 broadcast_multiply_fusion
  1720.6 4.7 fusion.10
  (11 shorter events, 0.2 us)
Async XLA Ops:
  7.2 820.9 %all-gather.4.cloned.1.call-start = ((), (), s32[]{:S(2)}) async-start(), calls=%async_computation.3 | async-start | bytes 4202496 | tf_op jit(solution)/shard_map/all_gather | solution.py:42
  13.7 3.2 copy-start
  17.9 71.4 %all-to-all-start.1 = ((bf16[16,2,512]{2,1,0:T(2,128)(2,1)}), bf16[16,2,512]{2,1,0:T(2,128)(2,1)S(1)}, u32[]{:S(2)}, u32[]{:S(2)}) async-start(bf16[16,2,512]{2,1,0:T(2,128)(2,1)} %reshape.276), calls=%async_computation.1 | async-start | bytes 65536 | tf_op jit(solution)/shard_map/all_to_all | solution.py:93
  43.7 1.2 copy-start.2
  89.3 740.8 %all-to-all-start = ((bf16[16,2,65536]{2,1,0:T(2,128)(2,1)}), bf16[16,2,65536]{2,1,0:T(2,128)(2,1)}, u32[]{:S(2)}, u32[]{:S(2)}) async-start(bf16[16,2,65536]{2,1,0:T(2,128)(2,1)} %reshape.278), calls=%async_computation | async-start | bytes 8388608 | tf_op jit(solution)/shard_map/all_to_all | solution.py:92
  96.5 1509.8 %all-gather.6.cloned.1.call-start = ((), (), s32[]{:S(2)}) async-start(), calls=%async_computation.4 | async-start | bytes 4456448 | tf_op jit(solution)/shard_map/all_gather | solution.py:66
  857.1 26.5 %copy-start.5 = (bf16[4,8]{1,0:T(4,128)(2,1)S(1)}, bf16[4,8]{1,0:T(4,128)(2,1)}, u32[]{:S(2)}) copy-start(bf16[4,8]{1,0:T(4,128)(2,1)} %param.9) | copy-start | bytes 196
  876.0 721.8 %all-to-all-start.2 = ((f32[4,32,1024]{2,0,1:T(4,128)}), f32[4,32,1024]{2,0,1:T(4,128)S(1)}, u32[]{:S(2)}, u32[]{:S(2)}) async-start(f32[4,32,1024]{2,0,1:T(4,128)} %copy.41), calls=%async_computation.2 | async-start | bytes 1048576 | tf_op jit(solution)/shard_map/all_to_all | solution.py:100
  1598.6 5.7 copy-start.1
  1598.6 5.7 copy-start.4
  1606.3 5.6 copy-start.3
Sparse Core Ops, SparseCore 0:
  10.1 817.8 all-gather.3
  831.4 63.5 all-gather.5
where the time goes:
time: 1730 us
  blocking collectives  818 us (47%)
  waiting for transfers between devices  732 us (42%)
  local copies, waits for them, and re-layouts  87.6 us (5%)
  other arithmetic  45.8 us (3%)
  starting transfers between devices  25 us (1%)
    all_gather x1, waiting for transfers between devices, local(): lax.all_gather(w_codes, ('node', 'local'), axis=1, tiled=True)  731 us
    all_gather x1, blocking collectives, local(): lax.all_gather(w_scales, ('node', 'local'), axis=1, tiled=True)  694 us
    psum x1, blocking collectives, local(): lax.psum(jnp.sum(normalized_grad * input_normalized, axis=0), ('node', 'l...  105 us
    unnamed x18, local copies, waits for them, and re-layouts  41.6 us
  transfers between devices with their start and end apart: 5, of which 1 were waited for; matrix products, arithmetic and copies ran while one was open for 7% of the time, Pallas kernels for 0%

commit v1 on v0

v1 whole, which is shorter than its diff:
```python
import functools
import math

import jax
import jax.numpy as jnp
from jax import lax
from jax.experimental import pallas as pl
from jax.experimental.pallas import tpu as pltpu
from jax.sharding import PartitionSpec as P

SEQ_LEN = 64
HALF = 256
TILE = 512
MESH = pl.DeviceIdType.MESH
F32 = jnp.float32
BF16 = jnp.bfloat16


def kernel(
    Z, inverse,
    cnt, tok, kg, wsh, g16,
    keys, tig, wg, gg,
    W, M, G, GR, W16, wrecv,
    yA, yB, yL, yR, S2, xA, xB, xL, xR, S3, zr, S4, wgr,
    qs, qz, qy, qyr, qx, qxr, qc, qcr,
    ag_s, ag_r, gz_s, gz_r, rz_s, rz_r, qz_s, qz_r, cr_s, cr_r, ms_s, ms_r,
):
    D = tok.shape[1]
    tiles = D // TILE
    zt = Z // tiles
    hz = Z // 2
    node = lax.axis_index("node")
    loc = lax.axis_index("local")
    z, xlo = node // 2, node % 2
    y, xhi, c = loc // 4, (loc // 2) % 2, loc % 2
    x = 2 * xhi + xlo
    sib = 1 - c

    def at_z(o):
        return (((z + o) % Z) * 2 + xlo, loc)

    def at_y(o):
        return (node, ((y + o) % 4) * 4 + xhi * 2 + c)

    def at_x(o):
        xx = (x + o) % 4
        return (z * 2 + xx % 2, y * 4 + (xx // 2) * 2 + c)

    at_core = (node, y * 4 + xhi * 2 + sib)

    def copy(src, dst, ss, rs_, dev):
        return pltpu.make_async_remote_copy(
            src_ref=src, dst_ref=dst, send_sem=ss, recv_sem=rs_,
            device_id=dev, device_id_type=MESH,
        )

    yp, ym, yo = (y + 1) % 4, (y + 3) % 4, (y + 2) % 4
    xs = [((x + o) % 4) % 2 for o in range(4)]
    xh = [((x + o) % 4) // 2 for o in range(4)]
    zA, zB = pl.ds(0, hz), pl.ds(hz, hz)

    barrier = pltpu.get_barrier_semaphore()

    def hello(o, carry):
        pl.semaphore_signal(barrier, inc=1, device_id=at_z(o), device_id_type=MESH)
        return carry

    lax.fori_loop(1, Z, hello, 0)
    for o in (1, 2, 3):
        pl.semaphore_signal(barrier, inc=1, device_id=at_y(o), device_id_type=MESH)
        pl.semaphore_signal(barrier, inc=1, device_id=at_x(o), device_id_type=MESH)
    pl.semaphore_signal(barrier, inc=1, device_id=at_core, device_id_type=MESH)

    def square(k, acc):
        t = tok[:, pl.ds(pl.multiple_of(k * TILE, TILE), TILE)].astype(F32)
        return acc + jnp.sum(t * t, axis=1, keepdims=True)

    total = lax.fori_loop(0, tiles, square, jnp.zeros((tok.shape[0], 1), F32))
    rs = lax.rsqrt(total / D + 1e-05)
    live = lax.broadcasted_iota(jnp.int32, (tok.shape[0], 1), 0) // SEQ_LEN < cnt[0]
    for h in range(2):
        m = jnp.where(live, kg[:, h * HALF:(h + 1) * HALF].astype(F32), 0.0)
        M[h] = (m * rs).astype(BF16)

    pl.semaphore_wait(barrier, Z - 1 + 7)

    wx = copy(wsh.at[sib], wrecv, ms_s.at[0], ms_r.at[0], at_core)
    wx.start()
    wx.wait()
    own, other = wsh[c], wrecv[...]
    W16[0:8, :] = jnp.where(c == 0, own, other)
    W16[8:16, :] = jnp.where(c == 0, other, own)
    W[c, z, xlo, y, xhi] = (W16[...] * g16[...]).astype(BF16)

    def agz(o, src_z):
        blk = W.at[c, src_z, xlo, y, xhi]
        return copy(blk, blk, gz_s.at[o], gz_r.at[o], at_z(o))

    def agz_start(o, carry):
        agz(o, z).start()
        return carry

    lax.fori_loop(1, Z, agz_start, 0)

    def core_copy(k):
        part = pl.ds(k * zt, zt)
        return copy(G.at[sib, part], GR.at[part], cr_s.at[k], cr_r.at[k], at_core)

    def grad(k, carry):
        t = tok[:, pl.ds(pl.multiple_of(k * TILE, TILE), TILE)]
        for h in range(2):
            g = lax.dot_general(t, M[h], (((0,), (0,)), ((), ())), preferred_element_type=F32)
            G[h, pl.ds(k * zt, zt)] = g.astype(BF16).reshape(zt, 2, 4, 2, 16, HALF)
        core_copy(k).start()
        return carry

    lax.fori_loop(0, tiles, grad, 0)

    def core_add(k, carry):
        core_copy(k).wait_recv()
        part = pl.ds(k * zt, zt)
        G[c, part] = (G[c, part].astype(F32) + GR[part].astype(F32)).astype(BF16)
        return carry

    y_a = copy(G.at[c, zA, :, yo], yA, ms_s.at[1], ms_r.at[1], at_y(1))
    y_b = copy(G.at[c, zB, :, yo], yB, ms_s.at[2], ms_r.at[2], at_y(3))
    y_l0 = copy(G.at[c, zA, :, yp], yL.at[zA], ms_s.at[3], ms_r.at[3], at_y(1))
    y_l1 = copy(G.at[c, zB, :, yp], yL.at[zB], ms_s.at[4], ms_r.at[4], at_y(1))
    y_r0 = copy(G.at[c, zA, :, ym], yR.at[zA], ms_s.at[5], ms_r.at[5], at_y(3))
    y_r1 = copy(G.at[c, zB, :, ym], yR.at[zB], ms_s.at[6], ms_r.at[6], at_y(3))
    lax.fori_loop(0, tiles // 2, core_add, 0)
    y_a.start()
    y_r0.start()
    lax.fori_loop(tiles // 2, tiles, core_add, 0)
    y_b.start()
    y_l1.start()

    def agz_wait(o, carry):
        agz(o, (z + Z - o) % Z).wait_recv()
        return carry

    lax.fori_loop(1, Z, agz_wait, 0)

    def agy(i, yy, o, half=None):
        blk = W.at[c, pl.ds(0, Z) if half is None else half, xlo, yy, xhi]
        return copy(blk, blk, ag_s.at[i], ag_r.at[i], at_y(o))

    agy(0, y, 1).start()
    agy(1, y, 3).start()

    def add_ya(k, carry):
        G[c, k, :, yp] = (G[c, k, :, yp].astype(F32) + yA[k].astype(F32)).astype(BF16)
        return carry

    def add_yb(k, carry):
        G[c, hz + k, :, ym] = (G[c, hz + k, :, ym].astype(F32) + yB[k].astype(F32)).astype(BF16)
        return carry

    y_a.wait_recv()
    lax.fori_loop(0, hz, add_ya, 0)
    y_l0.start()
    y_b.wait_recv()
    lax.fori_loop(0, hz, add_yb, 0)
    y_r1.start()

    agy(0, ym, 1).wait_recv()
    agy(2, ym, 1, zA).start()
    agy(1, yp, 3).wait_recv()
    agy(3, yp, 3, zB).start()
    agy(2, yo, 1, zA).wait_recv()
    agy(3, yo, 3, zB).wait_recv()

    def agx(i, o_src, o, half=None):
        blk = W.at[c, pl.ds(0, Z) if half is None else half, xs[o_src], :, xh[o_src]]
        return copy(blk, blk, ag_s.at[i], ag_r.at[i], at_x(o))

    def agc(i, o_src, h):
        blk = W.at[h, :, xs[o_src], :, xh[o_src]]
        return copy(blk, blk, ag_s.at[i], ag_r.at[i], at_core)

    agx(4, 0, 1).start()
    agx(5, 0, 3).start()
    agc(8, 0, c).start()

    y_r0.wait_recv()
    y_l1.wait_recv()
    y_l0.wait_recv()
    y_r1.wait_recv()

    def add_y(k, carry):
        S2[k] = (G[c, k, :, y].astype(F32) + yL[k].astype(F32) + yR[k].astype(F32)).astype(BF16)
        return carry

    lax.fori_loop(0, Z, add_y, 0)

    x_a = copy(S2.at[zA, xs[2], xh[2]], xA, ms_s.at[7], ms_r.at[7], at_x(1))
    x_b = copy(S2.at[zB, xs[2], xh[2]], xB, ms_s.at[8], ms_r.at[8], at_x(3))
    x_l0 = copy(S2.at[zA, xs[1], xh[1]], xL.at[zA], ms_s.at[9], ms_r.at[9], at_x(1))
    x_l1 = copy(S2.at[zB, xs[1], xh[1]], xL.at[zB], ms_s.at[10], ms_r.at[10], at_x(1))
    x_r0 = copy(S2.at[zA, xs[3], xh[3]], xR.at[zA], ms_s.at[11], ms_r.at[11], at_x(3))
    x_r1 = copy(S2.at[zB, xs[3], xh[3]], xR.at[zB], ms_s.at[12], ms_r.at[12], at_x(3))
    x_a.start()
    x_b.start()
    x_l1.start()
    x_r0.start()

    agx(4, 3, 1).wait_recv()
    agx(6, 3, 1, zA).start()
    agc(9, 3, c).start()
    agx(5, 1, 3).wait_recv()
    agx(7, 1, 3, zB).start()
    agc(10, 1, c).start()

    def add_xa(k, carry):
        S2[k, xs[1], xh[1]] = (S2[k, xs[1], xh[1]].astype(F32) + xA[k].astype(F32)).astype(BF16)
        return carry

    def add_xb(k, carry):
        S2[hz + k, xs[3], xh[3]] = (S2[hz + k, xs[3], xh[3]].astype(F32) + xB[k].astype(F32)).astype(BF16)
        return carry

    x_a.wait_recv()
    lax.fori_loop(0, hz, add_xa, 0)
    x_l0.start()
    x_b.wait_recv()
    lax.fori_loop(0, hz, add_xb, 0)
    x_r1.start()
    x_r0.wait_recv()
    x_l1.wait_recv()
    x_l0.wait_recv()
    x_r1.wait_recv()

    def add_x(k, carry):
        S3[k] = (S2[k, xlo, xhi].astype(F32) + xL[k].astype(F32) + xR[k].astype(F32)).astype(BF16)
        return carry

    lax.fori_loop(0, Z, add_x, 0)

    def rsz(o, dst_z, src_z):
        return copy(S3.at[dst_z], zr.at[src_z], rz_s.at[o], rz_r.at[o], at_z(o))

    def rsz_start(o, carry):
        rsz(o, (z + o) % Z, z).start()
        return carry

    lax.fori_loop(1, Z, rsz_start, 0)

    agx(6, 2, 1, zA).wait_recv()
    agx(7, 2, 3, zB).wait_recv()
    agc(11, 2, c).start()

    def rsz_add(o, acc):
        src = (z + Z - o) % Z
        rsz(o, z, src).wait_recv()
        return acc + zr[src].astype(F32)

    s4 = lax.fori_loop(1, Z, rsz_add, S3[z].astype(F32))

    q = jnp.sum(W16[...] * s4, axis=1, keepdims=True) * inverse
    s4 = s4 * (g16[...] * inverse)
    S4[0] = s4[0:8]
    S4[1] = s4[8:16]
    gx = copy(S4.at[sib], wgr, ms_s.at[13], ms_r.at[13], at_core)
    gx.start()
    lane = lax.broadcasted_iota(jnp.int32, (16, 128), 1)
    sub = lax.broadcasted_iota(jnp.int32, (16, 128), 0)
    row = jnp.sum(jnp.where(lane == (y * 2 + xhi) * 16 + sub, q, 0.0), axis=0, keepdims=True)
    sub8 = lax.broadcasted_iota(jnp.int32, (8, 128), 0)
    qs[...] = jnp.where(sub8 == (z * 2 + xlo) % 8, row, 0.0)
    qz[z] = qs[...]

    def gqz(o, src_z):
        return copy(qs, qz.at[src_z], qz_s.at[o], qz_r.at[o], at_z(o))

    def gqz_start(o, carry):
        gqz(o, z).start()
        return carry

    lax.fori_loop(1, Z, gqz_start, 0)

    for o in range(4):
        agc(8 + (0, 2, 3, 1)[o], o, sib).wait_recv()

    def project(k, acc):
        t = tok[:, pl.ds(pl.multiple_of(k * TILE, TILE), TILE)]
        return tuple(
            acc[h] + jnp.dot(t, W[h, pl.ds(k * zt, zt)].reshape(TILE, HALF), preferred_element_type=F32)
            for h in range(2)
        )

    zero = jnp.zeros((tok.shape[0], HALF), F32)
    prods = lax.fori_loop(0, tiles, project, (zero, zero))
    mean = jnp.zeros((tok.shape[0], 1), F32)
    for h in range(2):
        kf = jnp.where(live, prods[h] * rs, 0.0)
        keys[:, h * HALF:(h + 1) * HALF] = kf.astype(BF16)
        mean += jnp.sum(kf * kg[:, h * HALF:(h + 1) * HALF].astype(F32), axis=1, keepdims=True)
    coef = rs * rs * (mean / D)

    def back(k, carry):
        cols = pl.ds(pl.multiple_of(k * TILE, TILE), TILE)
        d = -(tok[:, cols].astype(F32) * coef)
        for h in range(2):
            d += lax.dot_general(
                M[h], W[h, pl.ds(k * zt, zt)].reshape(TILE, HALF),
                (((1,), (1,)), ((), ())), preferred_element_type=F32,
            )
        tig[:, cols] = d.astype(BF16)
        return carry

    def gqz_wait(o, carry):
        gqz(o, (z + Z - o) % Z).wait_recv()
        return carry

    lax.fori_loop(1, Z, gqz_wait, 0)
    for b in range(Z // 4):
        qy[b * 8:(b + 1) * 8, :] = qz[4 * b] + qz[4 * b + 1] + qz[4 * b + 2] + qz[4 * b + 3]
    qys = [copy(qy, qyr.at[o], ms_s.at[13 + o], ms_r.at[13 + o], at_y(o)) for o in (1, 2, 3)]
    for d in qys:
        d.start()
    lax.fori_loop(0, tiles // 2, back, 0)
    for d in qys:
        d.wait_recv()
    qx[...] = qy[...] + qyr[1] + qyr[2] + qyr[3]
    qxs = [copy(qx, qxr.at[o], ms_s.at[16 + o], ms_r.at[16 + o], at_x(o)) for o in (1, 2, 3)]
    for d in qxs:
        d.start()
    lax.fori_loop(tiles // 2, tiles, back, 0)
    for d in qxs:
        d.wait_recv()
    qc[...] = qx[...] + qxr[1] + qxr[2] + qxr[3]
    qcs = copy(qc, qcr, ms_s.at[20], ms_r.at[20], at_core)
    qcs.start()

    gx.wait_recv()
    own, other = S4[c], wgr[...]
    wg[:, 0:HALF] = jnp.where(c == 0, own, other)
    wg[:, HALF:2 * HALF] = jnp.where(c == 0, other, own)
    qcs.wait_recv()
    gg[...] = qc[...] + qcr[...]

    def sent_z(o, carry):
        agz(o, z).wait_send()
        rsz(o, (z + o) % Z, z).wait_send()
        gqz(o, z).wait_send()
        return carry

    lax.fori_loop(1, Z, sent_z, 0)

    def sent_core(k, carry):
        core_copy(k).wait_send()
        return carry

    lax.fori_loop(0, tiles, sent_core, 0)
    for d in (
        y_a, y_b, y_l0, y_l1, y_r0, y_r1, x_a, x_b, x_l0, x_l1, x_r0, x_r1, gx, qcs, *qys, *qxs,
        agy(0, y, 1), agy(1, y, 3), agy(2, ym, 1, zA), agy(3, yp, 3, zB),
        agx(4, 0, 1), agx(5, 0, 3), agx(6, 3, 1, zA), agx(7, 1, 3, zB),
        agc(8, 0, c), agc(9, 3, c), agc(10, 1, c), agc(11, 2, c),
    ):
        d.wait_send()


def local(tokens, gain, w_codes, w_scales, seq_counts, key_grad):
    rows, D = tokens.shape
    node_count = lax.axis_size("node")
    local_count = lax.axis_size("local")
    Z = node_count // 2
    inverse = 1.0 / math.sqrt(rows * node_count * local_count)
    chip = (lax.axis_index("node") * local_count + lax.axis_index("local")) // 2
    g16 = lax.dynamic_slice_in_dim(gain, chip * 16, 16, 0).reshape(16, 1)
    wsh = w_codes.astype(F32) * w_scales.astype(F32)[:, :, None]
    wsh = wsh.reshape(2, 2, 8, 128).transpose(0, 2, 1, 3).reshape(2, 8, HALF)
    vmem = pl.BlockSpec(memory_space=pltpu.VMEM)
    dma = pltpu.SemaphoreType.DMA
    hz = Z // 2
    keys, tig, wg, gg = pl.pallas_call(
        functools.partial(kernel, Z, inverse),
        out_shape=(
            jax.ShapeDtypeStruct((rows, 2 * HALF), BF16),
            jax.ShapeDtypeStruct((rows, D), BF16),
            jax.ShapeDtypeStruct((8, 2 * HALF), F32),
            jax.ShapeDtypeStruct((2 * Z, 128), F32),
        ),
        in_specs=[pl.BlockSpec(memory_space=pltpu.SMEM)] + [vmem] * 4,
        out_specs=(vmem,) * 4,
        scratch_shapes=[
            pltpu.VMEM((2, Z, 2, 4, 2, 16, HALF), BF16),
            pltpu.VMEM((2, rows, HALF), BF16),
            pltpu.VMEM((2, Z, 2, 4, 2, 16, HALF), BF16),
            pltpu.VMEM((Z, 2, 4, 2, 16, HALF), BF16),
            pltpu.VMEM((16, HALF), F32),
            pltpu.VMEM((8, HALF), F32),
            pltpu.VMEM((hz, 2, 2, 16, HALF), BF16),
            pltpu.VMEM((hz, 2, 2, 16, HALF), BF16),
            pltpu.VMEM((Z, 2, 2, 16, HALF), BF16),
            pltpu.VMEM((Z, 2, 2, 16, HALF), BF16),
            pltpu.VMEM((Z, 2, 2, 16, HALF), BF16),
            pltpu.VMEM((hz, 16, HALF), BF16),
            pltpu.VMEM((hz, 16, HALF), BF16),
            pltpu.VMEM((Z, 16, HALF), BF16),
            pltpu.VMEM((Z, 16, HALF), BF16),
            pltpu.VMEM((Z, 16, HALF), BF16),
            pltpu.VMEM((Z, 16, HALF), BF16),
            pltpu.VMEM((2, 8, HALF), F32),
            pltpu.VMEM((8, HALF), F32),
            pltpu.VMEM((8, 128), F32),
            pltpu.VMEM((Z, 8, 128), F32),
            pltpu.VMEM((2 * Z, 128), F32),
            pltpu.VMEM((4, 2 * Z, 128), F32),
            pltpu.VMEM((2 * Z, 128), F32),
            pltpu.VMEM((4, 2 * Z, 128), F32),
            pltpu.VMEM((2 * Z, 128), F32),
            pltpu.VMEM((2 * Z, 128), F32),
            dma((12,)), dma((12,)),
            dma((Z,)), dma((Z,)),
            dma((Z,)), dma((Z,)),
            dma((Z,)), dma((Z,)),
            dma((D // TILE,)), dma((D // TILE,)),
            dma((21,)), dma((21,)),
        ],
        compiler_params=pltpu.CompilerParams(
            collective_id=0, has_side_effects=True, vmem_limit_bytes=48 << 20
        ),
    )(seq_counts, tokens, key_grad, wsh, g16)
    return keys, tig, wg, gg.reshape(D)


def solution(mesh):
    return jax.shard_map(
        local,
        mesh=mesh,
        in_specs=(
            P(("node", "local"), None),
            P(),
            P(None, ("node", "local"), None),
            P(None, ("node", "local")),
            P(("node", "local")),
            P(("node", "local"), None),
        ),
        out_specs=(
            P(("node", "local"), None),
            P(("node", "local"), None),
            P(("node", "local"), None),
            P(),
        ),
        check_vma=False,
    )
```

time: 1730 us -> 108 us (0.06)
  blocking collectives: 818 us -> 0 us
  waiting for transfers between devices: 732 us -> 0 us
  Pallas kernels: 0 us -> 98.6 us
  local copies, waits for them, and re-layouts: 87.6 us -> 5.98 us
  other arithmetic: 45.8 us -> 1.45 us
  starting transfers between devices: 25 us -> 0 us
    all_gather x2 -> x0, waiting for transfers between devices: 731 us -> none  [the longest x1 731 us: local(): lax.all_gather(w_codes, ('node', 'local'), axis=1, tiled=True)]
    all_gather x2 -> x0, blocking collectives: 713 us -> none  [the longest x1 694 us: local(): lax.all_gather(w_scales, ('node', 'local'), axis=1, tiled=True)]
    psum x1 -> x0, blocking collectives: 105 us -> none  [local(): lax.psum(jnp.sum(normalized_grad * input_normalized, axis=0), ('node', 'l...]
    pallas_call x0 -> x1, Pallas kernels: none -> 98.6 us  [local(): pl.pallas_call(functools.partial(kernel, Z, inverse), out_shape=(jax.Shap...]
    unnamed x18 -> x10, local copies, waits for them, and re-layouts: 41.6 us -> 5.83 us
    another operation x6 -> x0, local copies, waits for them, and re-layouts: 26.7 us -> none  [quantize_blocks(): return (jnp.stack(code_list, axis=0), jnp.stack(scale_list, axis=0))]
    all_to_all x3 -> x0, starting transfers between devices: 24.9 us -> none  [the longest x1 10.2 us: local(): lax.all_to_all(scales_flat, 'local', split_axis=2, concat_axis=0, tiled=T...]
    convert_element_type x9 -> x1, other arithmetic: 21.6 us -> 0.68 us  [local(): wsh = w_codes.astype(F32) * w_scales.astype(F32)[:, :, None]]
  transfers between devices with their start and end apart: 5 -> 0, of which waited for: 1 -> 0; matrix products, arithmetic and copies ran while one was open for 7% -> 0% of each run, Pallas kernels for 0% -> 0%
where the time goes in v1:
time: 108 us; the launch traced here: 107 us
  Pallas kernels  98.6 us (91%)
  local copies, waits for them, and re-layouts  5.98 us (6%)
  other arithmetic  1.45 us (1%)
  between operations  1.32 us (1%)
    pallas_call x1, Pallas kernels, local(): pl.pallas_call(functools.partial(kernel, Z, inverse), out_shape=(jax.Shap...  98.6 us
    unnamed x10, local copies, waits for them, and re-layouts  5.83 us

profile of v1, /device:TPU:1, one launch (start us, length us, event | category | flops | bytes accessed | tf_op | source)
XLA Modules:
  0.0 107.3 jit_solution(11329408330414525772)
XLA Ops:
  0.6 0.0 copy-start
  1.3 0.0 copy-done
  1.4 0.1 dynamic-slice_bitcast_fusion
  1.4 0.7 convert_element_type.7
  2.1 0.1 copy.10.g16
  2.2 0.8 convert_multiply_fusion
  3.0 0.0 copy-start.1
  3.0 1.6 %copy-done.1 = bf16[256,4096]{1,0:T(8,128)(2,1)S(1)} copy-done((bf16[256,4096]{1,0:T(8,128)(2,1)S(1)}, bf16[256,4096]{1,0:T(8,128)(2,1)}, u32[]{:S(2)}) %copy-start.1) | copy-done | bytes 2097176
  4.6 0.0 copy-start.2
  4.6 0.9 copy-done.2
  5.5 98.6 %shard_map.93 = (bf16[256,512]{1,0:T(8,128)(2,1)S(1)}, bf16[256,4096]{1,0:T(8,128)(2,1)S(1)}, f32[8,512]{1,0:T(8,128)S(1)}, f32[32,128]{1,0:T(8,128)S(1)}) custom-call(s32[1]{0:T(128)S(6)} %copy.15.cnt, bf16[256,4096]{1,0:T(8,128)(2,1)S(1)} %copy-done.1, bf16[256,512]{1,0:T(8,128)(2,1)S(1)} %copy-done.2, f32[2,8,256]{2,1,0:T(8,128)S(1)} %bitcast.8, ...), custom_call_target="tpu_custom_call" | custom-call | tf_op jit(solution)/shard_map/pallas_call | solution.py:377
  104.1 0.7 copy.16
  104.8 1.3 %copy.17 = bf16[256,4096]{1,0:T(8,128)(2,1)} copy(bf16[256,4096]{1,0:T(8,128)(2,1)S(1)} %get-tuple-element.17) | data formatting | bytes 4194304
  106.1 0.6 copy.18
  106.7 0.6 copy.19
Async XLA Ops:
  0.6 0.7 copy-start
  3.0 1.6 %copy-start.1 = (bf16[256,4096]{1,0:T(8,128)(2,1)S(1)}, bf16[256,4096]{1,0:T(8,128)(2,1)}, u32[]{:S(2)}) copy-start(bf16[256,4096]{1,0:T(8,128)(2,1)} %tok.1) | copy-start | bytes 6291460
  4.6 0.9 copy-start.2

commit v2 on v1

v2 whole, which is shorter than its diff:
```python
import functools
import math

import jax
import jax.numpy as jnp
from jax import lax
from jax.experimental import pallas as pl
from jax.experimental.pallas import tpu as pltpu
from jax.sharding import PartitionSpec as P

SEQ_LEN = 64
HALF = 256
TILE = 512
MESH = pl.DeviceIdType.MESH
F32 = jnp.float32
BF16 = jnp.bfloat16
ALL = slice(None)


def copy(src, dst, send, recv, dev):
    return pltpu.make_async_remote_copy(
        src_ref=src, dst_ref=dst, send_sem=send, recv_sem=recv, device_id=dev, device_id_type=MESH
    )


class RingSum:
    def __init__(self, ref, at, first, n, bufs, sems, plus, minus):
        self.ref, self.at, self.first, self.n, self.h = ref, at, first, n, n // 2
        self.a, self.b, self.l, self.r = bufs
        h = self.h
        near, far = pl.ds(0, h), pl.ds(h, h)

        def one(i, o, part, dst, dev):
            src = ref.at[at(o, pl.ds(first + part.start, h))]
            return copy(src, dst, sems[0].at[i], sems[1].at[i], dev)

        self.to_a = one(0, 2, near, self.a, plus)
        self.to_b = one(1, 2, far, self.b, minus)
        self.l0 = one(2, 1, near, self.l.at[near], plus)
        self.l1 = one(3, 1, far, self.l.at[far], plus)
        self.r0 = one(4, 3, near, self.r.at[near], minus)
        self.r1 = one(5, 3, far, self.r.at[far], minus)
        self.copies = (self.to_a, self.to_b, self.l0, self.l1, self.r0, self.r1)

    def start(self):
        for d in (self.to_a, self.to_b, self.l1, self.r0):
            d.start()

    def add(self, o, base, buf):
        def body(k, carry):
            i = self.at(o, self.first + base + k)
            self.ref[i] = (self.ref[i].astype(F32) + buf[k].astype(F32)).astype(BF16)
            return carry

        lax.fori_loop(0, self.h, body, 0)

    def forward(self):
        self.to_a.wait_recv()
        self.add(1, 0, self.a)
        self.l0.start()
        self.to_b.wait_recv()
        self.add(3, self.h, self.b)
        self.r1.start()

    def finish(self, dst, dst_first):
        for d in (self.l1, self.r0, self.l0, self.r1):
            d.wait_recv()

        def body(k, carry):
            own = self.ref[self.at(0, self.first + k)].astype(F32)
            dst[dst_first + k] = (own + self.l[k].astype(F32) + self.r[k].astype(F32)).astype(BF16)
            return carry

        lax.fori_loop(0, self.n, body, 0)


class RingGather:
    def __init__(self, ref, at, first, n, sems, plus, minus):
        h = n // 2
        whole, near, far = pl.ds(first, n), pl.ds(first, h), pl.ds(first + h, h)

        def one(i, o, part, dev):
            block = ref.at[at(o, part)]
            return copy(block, block, sems[0].at[i], sems[1].at[i], dev)

        self.sends = (one(0, 0, whole, plus), one(1, 0, whole, minus), one(2, 3, near, plus), one(3, 1, far, minus))
        self.recvs = (one(0, 3, whole, plus), one(1, 1, whole, minus), one(2, 2, near, plus), one(3, 2, far, minus))

    def start(self):
        self.sends[0].start()
        self.sends[1].start()

    def pass_on(self, i):
        self.recvs[i].wait_recv()
        self.sends[2 + i].start()

    def finish(self):
        self.recvs[2].wait_recv()
        self.recvs[3].wait_recv()


def kernel(
    Z, inverse,
    cnt, tok_hbm, kg_hbm, codes, scales, gain,
    keys, tig, wg, gg,
    tok, kg, wsh, W, M, G, GR, W16, wrecv,
    ya, yb, yl, yr, xa, xb, xl, xr, Sy, Sx,
    ya2, yb2, yl2, yr2, xa2, xb2, xl2, xr2, S3, zr, S4, wgr,
    qs, qz, qy, qyr, qx, qxr,
    in_s, ag_s, ag_r, agc_s, agc_r, rs_s, rs_r, gz_s, gz_r, rz_s, rz_r, qz_s, qz_r, cr_s, cr_r, ms_s, ms_r,
):
    rows, D = tok.shape
    tiles = D // TILE
    zt = Z // tiles
    hz = Z // 2
    node = lax.axis_index("node")
    loc = lax.axis_index("local")
    z, xlo = node // 2, node % 2
    y, xhi, c = loc // 4, (loc // 2) % 2, loc % 2
    x = 2 * xhi + xlo
    sib = 1 - c

    def at_z(o):
        return (((z + o) % Z) * 2 + xlo, loc)

    def at_y(o):
        return (node, ((y + o) % 4) * 4 + xhi * 2 + c)

    def at_x(o, core):
        xx = (x + o) % 4
        return (z * 2 + xx % 2, y * 4 + (xx // 2) * 2 + core)

    at_core = (node, y * 4 + xhi * 2 + sib)
    ys = [(y + o) % 4 for o in range(4)]
    xs = [((x + o) % 4) % 2 for o in range(4)]
    xh = [((x + o) % 4) // 2 for o in range(4)]

    loads = [pltpu.make_async_copy(kg_hbm, kg, in_s.at[0])]
    for i in range(2):
        part = pl.ds(i * (D // 2), D // 2)
        loads.append(pltpu.make_async_copy(tok_hbm.at[:, part], tok.at[:, part], in_s.at[1 + i]))
    for d in loads:
        d.start()

    barrier = pltpu.get_barrier_semaphore()

    def greet(dev):
        pl.semaphore_signal(barrier, inc=1, device_id=dev, device_id_type=MESH)

    def hello(o, carry):
        greet(at_z(o))
        return carry

    greet(at_core)
    lax.fori_loop(1, Z, hello, 0)
    for o in (1, 2, 3):
        greet(at_y(o))
        greet(at_x(o, c))
        greet(at_x(o, sib))

    chip = (node * 16 + loc) // 2
    lane = lax.broadcasted_iota(jnp.int32, (16, 128), 1)
    sub = lax.broadcasted_iota(jnp.int32, (16, 128), 0)
    grow = gain[pl.ds(chip // 8, 1), :]
    g16 = jnp.sum(jnp.where(lane == (chip % 8) * 16 + sub, grow, 0.0), axis=1, keepdims=True)
    eye = lax.broadcasted_iota(jnp.int32, (8, 8), 0) == lax.broadcasted_iota(jnp.int32, (8, 8), 1)
    sc = scales[...].astype(F32)
    for b in range(4):
        col = jnp.sum(jnp.where(eye, sc[b:b + 1, :], 0.0), axis=1, keepdims=True)
        wsh[b // 2, :, (b % 2) * 128:(b % 2 + 1) * 128] = codes[b].astype(F32) * col

    pl.semaphore_wait(barrier, Z - 1 + 10)
    wx = copy(wsh.at[sib], wrecv, ms_s.at[0], ms_r.at[0], at_core)
    wx.start()

    def square(k, acc):
        t = tok[:, pl.ds(pl.multiple_of(k * TILE, TILE), TILE)].astype(F32)
        return acc + jnp.sum(t * t, axis=1, keepdims=True)

    loads[1].wait()
    total = lax.fori_loop(0, tiles // 2, square, jnp.zeros((rows, 1), F32))
    loads[2].wait()
    total = lax.fori_loop(tiles // 2, tiles, square, total)
    rs = lax.rsqrt(total / D + 1e-05)
    live = lax.broadcasted_iota(jnp.int32, (rows, 1), 0) // SEQ_LEN < cnt[0]
    loads[0].wait()
    for h in range(2):
        m = jnp.where(live, kg[:, h * HALF:(h + 1) * HALF].astype(F32), 0.0)
        M[h] = (m * rs).astype(BF16)

    wx.wait()
    own, other = wsh[c], wrecv[...]
    W16[0:8, :] = jnp.where(c == 0, own, other)
    W16[8:16, :] = jnp.where(c == 0, other, own)
    W[c, z, xlo, y, xhi] = (W16[...] * g16).astype(BF16)

    def agz(o, src_z):
        block = W.at[c, src_z, xlo, y, xhi]
        return copy(block, block, gz_s.at[o], gz_r.at[o], at_z(o))

    def agz_start(o, carry):
        agz(o, z).start()
        return carry

    lax.fori_loop(1, Z, agz_start, 0)

    def core_copy(k):
        part = pl.ds(k * zt, zt)
        return copy(G.at[sib, part], GR.at[part], cr_s.at[k], cr_r.at[k], at_core)

    def grad(k, carry):
        t = tok[:, pl.ds(pl.multiple_of(k * TILE, TILE), TILE)]
        for h in range(2):
            g = lax.dot_general(t, M[h], (((0,), (0,)), ((), ())), preferred_element_type=F32)
            G[h, pl.ds(k * zt, zt)] = g.astype(BF16).reshape(zt, 2, 4, 2, 16, HALF)
        core_copy(k).start()
        return carry

    lax.fori_loop(0, tiles, grad, 0)

    def core_add(k, carry):
        core_copy(k).wait_recv()
        part = pl.ds(k * zt, zt)
        G[c, part] = (G[c, part].astype(F32) + GR[part].astype(F32)).astype(BF16)
        return carry

    def sems(pair, i, n):
        return pair[0].at[pl.ds(i, n)], pair[1].at[pl.ds(i, n)]

    rsem = (rs_s, rs_r)
    sum_y = RingSum(
        G, lambda o, p: (c, p, ALL, ys[o]), 0, hz, (ya, yb, yl, yr), sems(rsem, 0, 6), at_y(1), at_y(3)
    )
    sum_x = RingSum(
        G, lambda o, p: (c, p, xs[o], ALL, xh[o]), hz, hz, (xa, xb, xl, xr), sems(rsem, 6, 6), at_x(1, c), at_x(3, c)
    )
    sum_yx = RingSum(
        Sy, lambda o, p: (p, xs[o], xh[o]), 0, hz, (xa2, xb2, xl2, xr2), sems(rsem, 12, 6), at_x(1, c), at_x(3, c)
    )
    sum_xy = RingSum(
        Sx, lambda o, p: (p, ys[o]), 0, hz, (ya2, yb2, yl2, yr2), sems(rsem, 18, 6), at_y(1), at_y(3)
    )
    asem = (ag_s, ag_r)
    get_y = RingGather(W, lambda o, p: (c, p, xlo, ys[o], xhi), 0, hz, sems(asem, 0, 4), at_y(1), at_y(3))
    get_x = RingGather(W, lambda o, p: (c, p, xs[o], y, xh[o]), hz, hz, sems(asem, 4, 4), at_x(1, c), at_x(3, c))
    get_yx = RingGather(W, lambda o, p: (c, p, xs[o], ALL, xh[o]), 0, hz, sems(asem, 8, 4), at_x(1, c), at_x(3, c))
    get_xy = RingGather(W, lambda o, p: (c, p, ALL, ys[o]), hz, hz, sems(asem, 12, 4), at_y(1), at_y(3))

    def hand_yx(o, half):
        block = W.at[half, pl.ds(0, hz), xs[o], :, xh[o]]
        return copy(block, block, agc_s.at[o], agc_r.at[o], at_core)

    def hand_xy(o, half):
        block = W.at[half, pl.ds(hz, hz), :, ys[o]]
        return copy(block, block, agc_s.at[4 + o], agc_r.at[4 + o], at_core)

    lax.fori_loop(0, tiles // 2, core_add, 0)
    sum_y.start()
    lax.fori_loop(tiles // 2, tiles, core_add, 0)
    sum_x.start()
    sum_y.forward()
    sum_x.forward()

    def agz_wait(o, carry):
        agz(o, (z + Z - o) % Z).wait_recv()
        return carry

    lax.fori_loop(1, Z, agz_wait, 0)
    get_y.start()
    get_x.start()
    sum_y.finish(Sy, 0)
    sum_yx.start()
    sum_x.finish(Sx, 0)
    sum_xy.start()
    for i in range(2):
        get_y.pass_on(i)
        get_x.pass_on(i)
    sum_yx.forward()
    sum_xy.forward()
    get_y.finish()
    get_yx.start()
    hand_yx(0, c).start()
    get_x.finish()
    get_xy.start()
    hand_xy(0, c).start()
    sum_yx.finish(S3, 0)
    sum_xy.finish(S3, hz)

    def rsz(o, dst_z, src_z):
        return copy(S3.at[dst_z], zr.at[src_z], rz_s.at[o], rz_r.at[o], at_z(o))

    def rsz_start(o, carry):
        rsz(o, (z + o) % Z, z).start()
        return carry

    lax.fori_loop(1, Z, rsz_start, 0)

    for i, o in ((0, 3), (1, 1)):
        get_yx.pass_on(i)
        hand_yx(o, c).start()
        get_xy.pass_on(i)
        hand_xy(o, c).start()

    def rsz_add(o, acc):
        src = (z + Z - o) % Z
        rsz(o, z, src).wait_recv()
        return acc + zr[src].astype(F32)

    s4 = lax.fori_loop(1, Z, rsz_add, S3[z].astype(F32))

    q = jnp.sum(W16[...] * s4, axis=1, keepdims=True) * inverse
    s4 = s4 * (g16 * inverse)
    S4[0] = s4[0:8]
    S4[1] = s4[8:16]
    gx = copy(S4.at[sib], wgr, ms_s.at[1], ms_r.at[1], at_core)
    gx.start()
    qs[...] = jnp.sum(jnp.where(lane == (y * 2 + xhi) * 16 + sub, q, 0.0), axis=0, keepdims=True)

    def gqz(o, src_z):
        return copy(qs, qz.at[src_z], qz_s.at[o], qz_r.at[o], at_z(o))

    def gqz_start(o, carry):
        gqz(o, z).start()
        return carry

    lax.fori_loop(1, Z, gqz_start, 0)

    get_yx.finish()
    hand_yx(2, c).start()
    get_xy.finish()
    hand_xy(2, c).start()

    zrow = lax.broadcasted_iota(jnp.int32, (Z, 128), 0)

    def gqz_add(o, acc):
        src = (z + Z - o) % Z
        gqz(o, src).wait_recv()
        return jnp.where(zrow == src, qz[src], acc)

    qy[...] = lax.fori_loop(1, Z, gqz_add, jnp.where(zrow == z, qs[...], 0.0))
    qys = [copy(qy, qyr.at[o], ms_s.at[1 + o], ms_r.at[1 + o], at_y(o)) for o in (1, 2, 3)]
    for d in qys:
        d.start()

    for o in range(4):
        hand_yx(o, sib).wait_recv()
        hand_xy(o, sib).wait_recv()
    span = D // 2

    def project(k, acc):
        t = tok[:, pl.ds(pl.multiple_of(k * span, span), span)]
        return tuple(
            acc[h] + jnp.dot(t, W[h, pl.ds(k * hz, hz)].reshape(span, HALF), preferred_element_type=F32)
            for h in range(2)
        )

    zero = jnp.zeros((rows, HALF), F32)
    prods = lax.fori_loop(0, 2, project, (zero, zero))
    mean = jnp.zeros((rows, 1), F32)
    for h in range(2):
        kf = jnp.where(live, prods[h] * rs, 0.0)
        keys[:, h * HALF:(h + 1) * HALF] = kf.astype(BF16)
        mean += jnp.sum(kf * kg[:, h * HALF:(h + 1) * HALF].astype(F32), axis=1, keepdims=True)
    coef = rs * rs * (mean / D)

    for d in qys:
        d.wait_recv()
    qx[...] = qy[...] + qyr[1] + qyr[2] + qyr[3]
    qxs = [
        copy(qx, qxr.at[o, r], ms_s.at[5 + 2 * o + r], ms_r.at[5 + 2 * o + r], at_x(o, sib if r else c))
        for o in range(4) for r in range(2) if o or r
    ]
    for d in qxs:
        d.start()

    def back(k, carry):
        cols = pl.ds(pl.multiple_of(k * TILE, TILE), TILE)
        d = -(tok[:, cols].astype(F32) * coef)
        for h in range(2):
            d += lax.dot_general(
                M[h], W[h, pl.ds(k * zt, zt)].reshape(TILE, HALF),
                (((1,), (1,)), ((), ())), preferred_element_type=F32,
            )
        tig[:, cols] = d.astype(BF16)
        return carry

    lax.fori_loop(0, tiles, back, 0)

    gx.wait_recv()
    own, other = S4[c], wgr[...]
    wg[:, 0:HALF] = jnp.where(c == 0, own, other)
    wg[:, HALF:2 * HALF] = jnp.where(c == 0, other, own)
    for d in qxs:
        d.wait_recv()
    gg[xlo] = qx[...] + qxr[0, 1] + qxr[2, 0] + qxr[2, 1]
    gg[1 - xlo] = (qxr[1, 0] + qxr[1, 1]) + (qxr[3, 0] + qxr[3, 1])

    def sent_z(o, carry):
        agz(o, z).wait_send()
        rsz(o, (z + o) % Z, z).wait_send()
        gqz(o, z).wait_send()
        return carry

    lax.fori_loop(1, Z, sent_z, 0)

    def sent_core(k, carry):
        core_copy(k).wait_send()
        return carry

    lax.fori_loop(0, tiles, sent_core, 0)
    for s in (sum_y, sum_x, sum_yx, sum_xy):
        for d in s.copies:
            d.wait_send()
    for s in (get_y, get_x, get_yx, get_xy):
        for d in s.sends:
            d.wait_send()
    for o in range(4):
        hand_yx(o, c).wait_send()
        hand_xy(o, c).wait_send()
    for d in (gx, *qys, *qxs):
        d.wait_send()


def local(tokens, gain, w_codes, w_scales, seq_counts, key_grad):
    rows, D = tokens.shape
    node_count = lax.axis_size("node")
    local_count = lax.axis_size("local")
    Z = node_count // 2
    inverse = 1.0 / math.sqrt(rows * node_count * local_count)
    vmem = pl.BlockSpec(memory_space=pltpu.VMEM)
    hbm = pl.BlockSpec(memory_space=pl.ANY)
    dma = pltpu.SemaphoreType.DMA
    hz = Z // 2

    def ring(n, *inner):
        return [pltpu.VMEM((m, *inner, 16, HALF), BF16) for m in (n // 2, n // 2, n, n)]

    keys, tig, wg, gg = pl.pallas_call(
        functools.partial(kernel, Z, inverse),
        out_shape=(
            jax.ShapeDtypeStruct((rows, 2 * HALF), BF16),
            jax.ShapeDtypeStruct((rows, D), BF16),
            jax.ShapeDtypeStruct((8, 2 * HALF), F32),
            jax.ShapeDtypeStruct((2, Z, 128), F32),
        ),
        in_specs=[pl.BlockSpec(memory_space=pltpu.SMEM), hbm, hbm, vmem, vmem, vmem],
        out_specs=(vmem,) * 4,
        scratch_shapes=[
            pltpu.VMEM((rows, D), BF16),
            pltpu.VMEM((rows, 2 * HALF), BF16),
            pltpu.VMEM((2, 8, HALF), F32),
            pltpu.VMEM((2, Z, 2, 4, 2, 16, HALF), BF16),
            pltpu.VMEM((2, rows, HALF), BF16),
            pltpu.VMEM((2, Z, 2, 4, 2, 16, HALF), BF16),
            pltpu.VMEM((Z, 2, 4, 2, 16, HALF), BF16),
            pltpu.VMEM((16, HALF), F32),
            pltpu.VMEM((8, HALF), F32),
            *ring(hz, 2, 2),
            *ring(hz, 4),
            pltpu.VMEM((hz, 2, 2, 16, HALF), BF16),
            pltpu.VMEM((hz, 4, 16, HALF), BF16),
            *ring(hz),
            *ring(hz),
            pltpu.VMEM((Z, 16, HALF), BF16),
            pltpu.VMEM((Z, 16, HALF), BF16),
            pltpu.VMEM((2, 8, HALF), F32),
            pltpu.VMEM((8, HALF), F32),
            pltpu.VMEM((1, 128), F32),
            pltpu.VMEM((Z, 1, 128), F32),
            pltpu.VMEM((Z, 128), F32),
            pltpu.VMEM((4, Z, 128), F32),
            pltpu.VMEM((Z, 128), F32),
            pltpu.VMEM((4, 2, Z, 128), F32),
            dma((3,)),
            dma((16,)), dma((16,)),
            dma((8,)), dma((8,)),
            dma((24,)), dma((24,)),
            dma((Z,)), dma((Z,)),
            dma((Z,)), dma((Z,)),
            dma((Z,)), dma((Z,)),
            dma((D // TILE,)), dma((D // TILE,)),
            dma((13,)), dma((13,)),
        ],
        compiler_params=pltpu.CompilerParams(
            collective_id=0, has_side_effects=True, vmem_limit_bytes=48 << 20
        ),
    )(seq_counts, tokens, key_grad, w_codes, w_scales, gain.reshape(D // 128, 128))
    return keys, tig, wg, gg.transpose(1, 0, 2).reshape(D)


def solution(mesh):
    return jax.shard_map(
        local,
        mesh=mesh,
        in_specs=(
            P(("node", "local"), None),
            P(),
            P(None, ("node", "local"), None),
            P(None, ("node", "local")),
            P(("node", "local")),
            P(("node", "local"), None),
        ),
        out_specs=(
            P(("node", "local"), None),
            P(("node", "local"), None),
            P(("node", "local"), None),
            P(),
        ),
        check_vma=False,
    )
```

time: 108 us -> 79 us (0.73)
  Pallas kernels: 98.6 us -> 69.6 us
  local copies, waits for them, and re-layouts: 5.98 us -> 7.87 us
  other arithmetic: 1.45 us -> 0 us
    pallas_call x1, Pallas kernels: 98.6 us -> 69.6 us  [local(): pl.pallas_call(functools.partial(kernel, Z, inverse), out_shape=(jax.Shap...]
    unnamed x10 -> x13, local copies, waits for them, and re-layouts: 5.83 us -> 7.25 us
where the time goes in v2:
time: 79 us; the launch traced here: 78.7 us
  Pallas kernels  69.6 us (88%)
  local copies, waits for them, and re-layouts  7.87 us (10%)
  between operations  1.3 us (2%)
    pallas_call x1, Pallas kernels, local(): pl.pallas_call(functools.partial(kernel, Z, inverse), out_shape=(jax.Shap...  69.6 us
    unnamed x13, local copies, waits for them, and re-layouts  7.25 us

profile of v2, /device:TPU:1, one launch (start us, length us, event | category | flops | bytes accessed | tf_op | source)
XLA Modules:
  0.0 78.7 jit_solution(851350902084796069)
XLA Ops:
  1.3 0.0 copy-start
  1.3 1.6 %copy-done = bf16[256,4096]{1,0:T(8,128)(2,1)S(1)} copy-done((bf16[256,4096]{1,0:T(8,128)(2,1)S(1)}, bf16[256,4096]{1,0:T(8,128)(2,1)}, u32[]{:S(2)}) %copy-start) | copy-done | bytes 2097176
  2.9 0.0 copy-start.1
  2.9 0.9 %copy-done.1 = bf16[256,512]{1,0:T(8,128)(2,1)S(1)} copy-done((bf16[256,512]{1,0:T(8,128)(2,1)S(1)}, bf16[256,512]{1,0:T(8,128)(2,1)}, u32[]{:S(2)}) %copy-start.1) | copy-done | bytes 262168
  3.8 0.0 copy-start.2
  3.8 0.7 copy-done.2
  4.5 0.0 copy-start.3
  4.5 0.7 copy-done.3
  5.2 0.0 copy-start.4
  5.2 0.7 copy-done.4
  5.9 69.6 %shard_map.93 = (bf16[256,512]{1,0:T(8,128)(2,1)S(1)}, bf16[256,4096]{1,0:T(8,128)(2,1)S(1)}, f32[8,512]{1,0:T(8,128)S(1)}, f32[2,16,128]{2,1,0:T(8,128)S(1)}) custom-call(s32[1]{0:T(128)S(6)} %copy.14.cnt, bf16[256,4096]{1,0:T(8,128)(2,1)S(1)} %copy-done, bf16[256,512]{1,0:T(8,128)(2,1)S(1)} %copy-done.1, bf16[4,8,128]{2,1,0:T(8,128)(2,1)S(1)} %copy-done.3, ...), custom_call_target="tpu_custom_call" | custom-call | tf_op jit(solution)/shard_map/pallas_call | solution.py:438
  75.5 0.6 copy.10
  76.1 0.7 copy.15
  76.8 1.3 %copy.16 = bf16[256,4096]{1,0:T(8,128)(2,1)} copy(bf16[256,4096]{1,0:T(8,128)(2,1)S(1)} %get-tuple-element.17) | data formatting | bytes 4194304
  78.1 0.6 copy.17
Async XLA Ops:
  1.3 1.6 %copy-start = (bf16[256,4096]{1,0:T(8,128)(2,1)S(1)}, bf16[256,4096]{1,0:T(8,128)(2,1)}, u32[]{:S(2)}) copy-start(bf16[256,4096]{1,0:T(8,128)(2,1)} %tok_hbm.1) | copy-start | bytes 6291460
  2.9 0.9 %copy-start.1 = (bf16[256,512]{1,0:T(8,128)(2,1)S(1)}, bf16[256,512]{1,0:T(8,128)(2,1)}, u32[]{:S(2)}) copy-start(bf16[256,512]{1,0:T(8,128)(2,1)} %kg_hbm.1) | copy-start | bytes 786436
  3.8 0.7 copy-start.2
  4.5 0.7 copy-start.3
  5.2 0.7 copy-start.4

commit v3 on v2

v3 whole, which is shorter than its diff:
```python
import functools
import math

import jax
import jax.numpy as jnp
from jax import lax
from jax.experimental import pallas as pl
from jax.experimental.pallas import tpu as pltpu
from jax.sharding import PartitionSpec as P

SEQ_LEN = 64
HALF = 256
TILE = 512
WIDE = 1024
MESH = pl.DeviceIdType.MESH
F32 = jnp.float32
BF16 = jnp.bfloat16
ALL = slice(None)
VMEM_BYTES = 63 << 20


def copy(src, dst, send, recv, dev):
    return pltpu.make_async_remote_copy(
        src_ref=src, dst_ref=dst, send_sem=send, recv_sem=recv, device_id=dev, device_id_type=MESH
    )


def settle(ref, send=None, recv=None, dev=None):
    d = copy(ref, ref, send if recv is None else recv, recv if send is None else send, dev)
    if recv is None:
        d.wait_send()
    else:
        d.wait_recv()


class RingSum:
    def __init__(self, ref, at, first, n, bufs, sems, plus, minus):
        self.ref, self.at, self.first, self.n, self.h = ref, at, first, n, n // 2
        self.a, self.b, self.lr = bufs
        self.send, self.recv, self.dev = *sems, plus
        h = self.h
        near, far = pl.ds(0, h), pl.ds(h, h)

        def one(i, o, part, dst, dev):
            src = ref.at[at(o, pl.ds(first + part.start, h))]
            return copy(src, dst, self.send, self.recv.at[i], dev)

        self.to_a = one(0, 2, near, self.a, plus)
        self.to_b = one(1, 2, far, self.b, minus)
        self.l0 = one(2, 1, near, self.lr.at[0, near], plus)
        self.l1 = one(2, 1, far, self.lr.at[0, far], plus)
        self.r0 = one(2, 3, near, self.lr.at[1, near], minus)
        self.r1 = one(2, 3, far, self.lr.at[1, far], minus)

    def start(self):
        for d in (self.to_a, self.to_b, self.l1, self.r0):
            d.start()

    def add(self, o, base, buf):
        def body(k, carry):
            i = self.at(o, self.first + base + k)
            self.ref[i] = (self.ref[i].astype(F32) + buf[k].astype(F32)).astype(BF16)
            return carry

        lax.fori_loop(0, self.h, body, 0)

    def forward(self):
        self.to_a.wait_recv()
        self.add(1, 0, self.a)
        self.l0.start()
        self.to_b.wait_recv()
        self.add(3, self.h, self.b)
        self.r1.start()

    def finish(self, dst, dst_first):
        settle(self.lr, recv=self.recv.at[2], dev=self.dev)

        def body(k, carry):
            own = self.ref[self.at(0, self.first + k)].astype(F32)
            total = own + self.lr[0, k].astype(F32) + self.lr[1, k].astype(F32)
            dst[dst_first + k] = total.astype(BF16)
            return carry

        lax.fori_loop(0, self.n, body, 0)

    def sent(self, like):
        settle(like, send=self.send, dev=self.dev)


class RingGather:
    def __init__(self, ref, at, first, n, sems, plus, minus):
        h = n // 2
        whole, near, far = pl.ds(first, n), pl.ds(first, h), pl.ds(first + h, h)
        self.send, self.recv, self.dev = *sems, plus
        self.opposite = ref.at[at(2, whole)]

        def one(i, o, part, dev):
            block = ref.at[at(o, part)]
            return copy(block, block, self.send, self.recv.at[i], dev)

        self.sends = (one(0, 0, whole, plus), one(1, 0, whole, minus), one(2, 3, near, plus), one(2, 1, far, minus))
        self.recvs = (one(0, 3, whole, plus), one(1, 1, whole, minus))

    def start(self):
        self.sends[0].start()
        self.sends[1].start()

    def pass_on(self, i):
        self.recvs[i].wait_recv()
        self.sends[2 + i].start()

    def finish(self):
        settle(self.opposite, recv=self.recv.at[2], dev=self.dev)

    def sent(self, like):
        settle(like, send=self.send, dev=self.dev)


def kernel(
    Z, inverse,
    cnt, tok_hbm, kg_hbm, codes_hbm, scales_hbm, gain_hbm,
    keys_hbm, tig_hbm, wg_hbm, gg_hbm,
    tok, kg, codes, scales, gain, keys, tig, wg, gg, wsh, W, M, G, GR, W16, wrecv,
    ya, yb, ylr, xa, xb, xlr, Sy, Sx,
    ya2, yb2, ylr2, xa2, xb2, xlr2, S3, zr, S4, wgr,
    qs, qz, qy, qyr, qx, qxr,
    in_s, out_s, ag_r, rs_r, cr_r, ms_s, ms_r,
):
    rows, D = tok.shape
    tiles = D // TILE
    zt = Z // tiles
    gtiles = D // WIDE
    gt = Z // gtiles
    hz = Z // 2
    node = lax.axis_index("node")
    loc = lax.axis_index("local")
    z, xlo = node // 2, node % 2
    y, xhi, c = loc // 4, (loc // 2) % 2, loc % 2
    x = 2 * xhi + xlo
    sib = 1 - c

    def at_z(o):
        return (((z + o) % Z) * 2 + xlo, loc)

    def at_y(o):
        return (node, ((y + o) % 4) * 4 + xhi * 2 + c)

    def at_x(o, core):
        xx = (x + o) % 4
        return (z * 2 + xx % 2, y * 4 + (xx // 2) * 2 + core)

    at_core = (node, y * 4 + xhi * 2 + sib)
    ys = [(y + o) % 4 for o in range(4)]
    xs = [((x + o) % 4) % 2 for o in range(4)]
    xh = [((x + o) % 4) // 2 for o in range(4)]

    loads = []
    for i in range(2):
        part = pl.ds(i * (D // 2), D // 2)
        loads.append(pltpu.make_async_copy(tok_hbm.at[:, part], tok.at[:, part], in_s.at[i]))
    for i, (a, b) in enumerate(((kg_hbm, kg), (codes_hbm, codes), (scales_hbm, scales), (gain_hbm, gain))):
        loads.append(pltpu.make_async_copy(a, b, in_s.at[2 + i]))
    for d in loads:
        d.start()

    barrier = pltpu.get_barrier_semaphore()

    def greet(dev):
        pl.semaphore_signal(barrier, inc=1, device_id=dev, device_id_type=MESH)

    def hello(o, carry):
        greet(at_z(o))
        return carry

    greet(at_core)
    lax.fori_loop(1, Z, hello, 0)
    for o in (1, 2, 3):
        greet(at_y(o))
        greet(at_x(o, c))
        greet(at_x(o, sib))

    for d in loads[3:]:
        d.wait()
    chip = (node * 16 + loc) // 2
    lane = lax.broadcasted_iota(jnp.int32, (16, 128), 1)
    sub = lax.broadcasted_iota(jnp.int32, (16, 128), 0)
    grow = gain[pl.ds(chip // 8, 1), :]
    g16 = jnp.sum(jnp.where(lane == (chip % 8) * 16 + sub, grow, 0.0), axis=1, keepdims=True)
    eye = lax.broadcasted_iota(jnp.int32, (8, 8), 0) == lax.broadcasted_iota(jnp.int32, (8, 8), 1)
    sc = scales[...].astype(F32)
    for b in range(4):
        col = jnp.sum(jnp.where(eye, sc[b:b + 1, :], 0.0), axis=1, keepdims=True)
        wsh[b // 2, :, (b % 2) * 128:(b % 2 + 1) * 128] = codes[b].astype(F32) * col

    def square(k, acc):
        for i in range(TILE // 128):
            t = tok[:, pl.ds(pl.multiple_of(k * TILE + i * 128, 128), 128)].astype(F32)
            acc += t * t
        return acc

    loads[0].wait()
    total = lax.fori_loop(0, tiles // 2, square, jnp.zeros((rows, 128), F32))
    loads[1].wait()
    total = lax.fori_loop(tiles // 2, tiles, square, total)
    pl.semaphore_wait(barrier, Z - 1 + 10)
    wx = copy(wsh.at[sib], wrecv, ms_s.at[1], ms_r.at[0], at_core)
    wx.start()

    rs = lax.rsqrt(jnp.sum(total, axis=1, keepdims=True) / D + 1e-05)
    live = lax.broadcasted_iota(jnp.int32, (rows, 1), 0) // SEQ_LEN < cnt[0]
    loads[2].wait()
    M[...] = (jnp.where(live, kg[...].astype(F32), 0.0) * rs).astype(BF16)

    def core_copy(k):
        part = pl.ds(k * gt, gt)
        return copy(G.at[sib, part], GR.at[part], ms_s.at[0], cr_r.at[k], at_core)

    def grad(k, carry):
        t = tok[:, pl.ds(pl.multiple_of(k * WIDE, WIDE), WIDE)]
        g = lax.dot_general(t, M[...], (((0,), (0,)), ((), ())), preferred_element_type=F32).astype(BF16)
        for h in range(2):
            G[h, pl.ds(k * gt, gt)] = g[:, h * HALF:(h + 1) * HALF].reshape(gt, 2, 4, 2, 16, HALF)
        core_copy(k).start()
        return carry

    lax.fori_loop(0, gtiles // 2, grad, 0)

    wx.wait_recv()
    own, other = wsh[c], wrecv[...]
    W16[0:8, :] = jnp.where(c == 0, own, other)
    W16[8:16, :] = jnp.where(c == 0, other, own)
    W[c, z, xlo, y, xhi] = (W16[...] * g16).astype(BF16)

    def agz(o, src_z):
        block = W.at[c, src_z, xlo, y, xhi]
        return copy(block, block, ms_s.at[2], ms_r.at[1], at_z(o))

    def agz_start(o, carry):
        agz(o, z).start()
        return carry

    lax.fori_loop(1, Z, agz_start, 0)

    lax.fori_loop(gtiles // 2, gtiles, grad, 0)

    def core_add(k, carry):
        core_copy(k).wait_recv()
        part = pl.ds(k * gt, gt)
        G[c, part] = (G[c, part].astype(F32) + GR[part].astype(F32)).astype(BF16)
        return carry

    def sems(i, pair, j, n):
        return ms_s.at[i], pair.at[pl.ds(j, n)]

    sum_y = RingSum(G, lambda o, p: (c, p, ALL, ys[o]), 0, hz, (ya, yb, ylr), sems(8, rs_r, 0, 3), at_y(1), at_y(3))
    sum_x = RingSum(
        G, lambda o, p: (c, p, xs[o], ALL, xh[o]), hz, hz, (xa, xb, xlr), sems(9, rs_r, 3, 3), at_x(1, c), at_x(3, c)
    )
    sum_yx = RingSum(
        Sy, lambda o, p: (p, xs[o], xh[o]), 0, hz, (xa2, xb2, xlr2), sems(10, rs_r, 6, 3), at_x(1, c), at_x(3, c)
    )
    sum_xy = RingSum(Sx, lambda o, p: (p, ys[o]), 0, hz, (ya2, yb2, ylr2), sems(11, rs_r, 9, 3), at_y(1), at_y(3))
    get_y = RingGather(W, lambda o, p: (c, p, xlo, ys[o], xhi), 0, hz, sems(12, ag_r, 0, 3), at_y(1), at_y(3))
    get_x = RingGather(W, lambda o, p: (c, p, xs[o], y, xh[o]), hz, hz, sems(13, ag_r, 3, 3), at_x(1, c), at_x(3, c))
    get_yx = RingGather(
        W, lambda o, p: (c, p, xs[o], ALL, xh[o]), 0, hz, sems(14, ag_r, 6, 3), at_x(1, c), at_x(3, c)
    )
    get_xy = RingGather(W, lambda o, p: (c, p, ALL, ys[o]), hz, hz, sems(15, ag_r, 9, 3), at_y(1), at_y(3))

    def hand_yx(o, half):
        block = W.at[half, pl.ds(0, hz), xs[o], :, xh[o]]
        return copy(block, block, ms_s.at[3], ms_r.at[2], at_core)

    def hand_xy(o, half):
        block = W.at[half, pl.ds(hz, hz), :, ys[o]]
        return copy(block, block, ms_s.at[3], ms_r.at[2], at_core)

    lax.fori_loop(0, gtiles // 2, core_add, 0)
    sum_y.start()
    lax.fori_loop(gtiles // 2, gtiles, core_add, 0)
    sum_x.start()

    sum_y.forward()
    sum_x.forward()

    settle(W.at[c, pl.ds(0, Z - 1), xlo, y, xhi], recv=ms_r.at[1], dev=at_core)
    get_y.start()
    get_x.start()
    sum_y.finish(Sy, 0)
    sum_yx.start()
    sum_x.finish(Sx, 0)
    sum_xy.start()
    for i in range(2):
        get_y.pass_on(i)
        get_x.pass_on(i)
    sum_yx.forward()
    sum_xy.forward()
    get_y.finish()
    get_yx.start()
    hand_yx(0, c).start()
    get_x.finish()
    get_xy.start()
    hand_xy(0, c).start()
    sum_yx.finish(S3, 0)
    sum_xy.finish(S3, hz)

    q = jnp.sum(W[c, :, xlo, y, xhi].astype(F32) * S3[...].astype(F32), axis=2, keepdims=True).reshape(Z * 16, 1)
    diag = lax.broadcasted_iota(jnp.int32, (Z * 16, Z * 16), 0) == lax.broadcasted_iota(jnp.int32, (Z * 16, Z * 16), 1)
    qs[...] = jnp.sum(jnp.where(diag, q, 0.0), axis=0, keepdims=True)

    def gqz(o, src_z):
        return copy(qs, qz.at[src_z], ms_s.at[5], ms_r.at[4], at_z(o))

    def gqz_start(o, carry):
        gqz(o, z).start()
        return carry

    lax.fori_loop(1, Z, gqz_start, 0)

    def rsz(o, dst_z, src_z):
        return copy(S3.at[dst_z], zr.at[src_z], ms_s.at[4], ms_r.at[3], at_z(o))

    def rsz_start(o, carry):
        rsz(o, (z + o) % Z, z).start()
        return carry

    lax.fori_loop(1, Z, rsz_start, 0)

    for i, o in ((0, 3), (1, 1)):
        get_yx.pass_on(i)
        hand_yx(o, c).start()
        get_xy.pass_on(i)
        hand_xy(o, c).start()

    def gqz_add(o, acc):
        src = (z + Z - o) % Z
        return acc + qz[src]

    settle(qz.at[pl.ds(0, Z - 1)], recv=ms_r.at[4], dev=at_core)
    qsum = lax.fori_loop(1, Z, gqz_add, qs[...])
    lane = lax.broadcasted_iota(jnp.int32, (Z, Z * 16), 1)
    zrow = lax.broadcasted_iota(jnp.int32, (Z, Z * 16), 0)
    spread = jnp.where((lane >= zrow * 16) & (lane < zrow * 16 + 16), qsum, 0.0)
    src = lax.broadcasted_iota(jnp.int32, (Z * 16, 128), 0)
    to = lax.broadcasted_iota(jnp.int32, (Z * 16, 128), 1)
    place = jnp.where((src & 15) + (y * 2 + xhi) * 16 == to, 1.0, 0.0)
    qy[...] = jnp.dot(spread, place, precision=lax.Precision.HIGHEST, preferred_element_type=F32)
    qys = [copy(qy, qyr.at[o], ms_s.at[6], ms_r.at[6], at_y(o)) for o in (1, 2, 3)]
    for d in qys:
        d.start()

    get_yx.finish()
    hand_yx(2, c).start()
    get_xy.finish()
    hand_xy(2, c).start()

    settle(qyr.at[pl.ds(0, 3)], recv=ms_r.at[6], dev=at_core)
    qx[...] = qy[...] + qyr[1] + qyr[2] + qyr[3]
    qxs = [
        copy(qx, qxr.at[2 * o + r], ms_s.at[7], ms_r.at[7], at_x(o, sib if r else c))
        for o in range(4) for r in range(2) if o or r
    ]
    for d in qxs:
        d.start()

    def rsz_add(o, acc):
        src = (z + Z - o) % Z
        return acc + zr[src].astype(F32)

    settle(zr.at[pl.ds(0, Z - 1)], recv=ms_r.at[3], dev=at_core)
    s4 = lax.fori_loop(1, Z, rsz_add, S3[z].astype(F32))

    s4 = s4 * (g16 * inverse)
    S4[0] = s4[0:8]
    S4[1] = s4[8:16]
    gx = copy(S4.at[sib], wgr, ms_s.at[1], ms_r.at[5], at_core)
    gx.start()

    settle(W.at[sib], recv=ms_r.at[2], dev=at_core)
    span = D // 2

    def project(k, acc):
        t = tok[:, pl.ds(pl.multiple_of(k * span, span), span)]
        return tuple(
            acc[h] + jnp.dot(t, W[h, pl.ds(k * hz, hz)].reshape(span, HALF), preferred_element_type=F32)
            for h in range(2)
        )

    zero = jnp.zeros((rows, HALF), F32)
    prods = lax.fori_loop(0, 2, project, (zero, zero))
    mean = jnp.zeros((rows, 1), F32)
    for h in range(2):
        kf = jnp.where(live, prods[h] * rs, 0.0)
        keys[:, h * HALF:(h + 1) * HALF] = kf.astype(BF16)
        mean += jnp.sum(kf * kg[:, h * HALF:(h + 1) * HALF].astype(F32), axis=1, keepdims=True)
    coef = rs * rs * (mean / D)
    stores = [
        pltpu.make_async_copy(a, b, out_s.at[i])
        for i, (a, b) in enumerate(((keys, keys_hbm), (wg, wg_hbm), (gg, gg_hbm)))
    ]
    stores[0].start()

    def back(k, carry):
        cols = pl.ds(pl.multiple_of(k * TILE, TILE), TILE)
        d = -(tok[:, cols].astype(F32) * coef)
        for h in range(2):
            d += lax.dot_general(
                M[:, h * HALF:(h + 1) * HALF], W[h, pl.ds(k * zt, zt)].reshape(TILE, HALF),
                (((1,), (1,)), ((), ())), preferred_element_type=F32,
            )
        tig[:, cols] = d.astype(BF16)
        pltpu.make_async_copy(tig.at[:, cols], tig_hbm.at[:, cols], out_s.at[3]).start()
        return carry

    lax.fori_loop(0, tiles, back, 0)

    gx.wait_recv()
    own, other = S4[c], wgr[...]
    wg[:, 0:HALF] = jnp.where(c == 0, own, other)
    wg[:, HALF:2 * HALF] = jnp.where(c == 0, other, own)
    stores[1].start()
    settle(qxr.at[pl.ds(0, 7)], recv=ms_r.at[7], dev=at_core)
    same = qx[...] + qxr[1] + qxr[4] + qxr[5]
    next_x = (qxr[2] + qxr[3]) + (qxr[6] + qxr[7])
    row = lax.broadcasted_iota(jnp.int32, (2 * Z, Z), 0)
    zcol = lax.broadcasted_iota(jnp.int32, (2 * Z, Z), 1)
    total = sum(
        jnp.dot(
            jnp.where(row == 2 * zcol + p, 1.0, 0.0), v,
            precision=lax.Precision.HIGHEST, preferred_element_type=F32,
        )
        for p, v in ((xlo, same), (1 - xlo, next_x))
    )
    gg[...] = total * inverse / gain[...]
    stores[2].start()

    wx.wait_send()
    gx.wait_send()
    for ref, i in (
        (G.at[sib], 0), (W.at[c, pl.ds(0, Z - 1), xlo, y, xhi], 2), (W.at[c], 3), (S3.at[pl.ds(0, Z - 1)], 4),
        (qz.at[pl.ds(0, Z - 1)], 5), (qyr.at[pl.ds(0, 3)], 6), (qxr.at[pl.ds(0, 7)], 7),
    ):
        settle(ref, send=ms_s.at[i], dev=at_core)
    sum_y.sent(G.at[c, pl.ds(0, hz), :, pl.ds(0, 3)])
    sum_x.sent(G.at[c, pl.ds(0, hz), :, pl.ds(0, 3)])
    sum_yx.sent(Sx.at[:, pl.ds(0, 3)])
    sum_xy.sent(Sx.at[:, pl.ds(0, 3)])
    get_y.sent(W.at[c, pl.ds(0, hz), xlo, pl.ds(0, 3), xhi])
    get_x.sent(W.at[c, pl.ds(0, hz), xlo, pl.ds(0, 3), xhi])
    get_yx.sent(W.at[c, pl.ds(0, hz), :, pl.ds(0, 3)])
    get_xy.sent(W.at[c, pl.ds(0, hz), :, pl.ds(0, 3)])
    pltpu.make_async_copy(tig, tig_hbm, out_s.at[3]).wait()
    for d in stores:
        d.wait()


def keep(keys, tig, wg, gg, keys_out, tig_out, wg_out, gg_out, keys_v, tig_v, wg_v, gg_v, in_s, out_s):
    step = tig.shape[0] // 4
    moves = [(keys, keys_v, keys_out), (wg, wg_v, wg_out), (gg, gg_v, gg_out)]
    for i in range(4):
        part = pl.ds(i * step, step)
        moves.append((tig.at[part], tig_v.at[part], tig_out.at[part]))
    reads = [pltpu.make_async_copy(a, v, in_s.at[i]) for i, (a, v, _) in enumerate(moves)]
    writes = [pltpu.make_async_copy(v, b, out_s.at[i]) for i, (_, v, b) in enumerate(moves)]
    for d in reads:
        d.start()
    for r, w in zip(reads, writes):
        r.wait()
        w.start()
    for w in writes:
        w.wait()


def local(tokens, gain, w_codes, w_scales, seq_counts, key_grad):
    rows, D = tokens.shape
    node_count = lax.axis_size("node")
    local_count = lax.axis_size("local")
    Z = node_count // 2
    inverse = 1.0 / math.sqrt(rows * node_count * local_count)
    hbm = pl.BlockSpec(memory_space=pl.ANY)
    dma = pltpu.SemaphoreType.DMA
    hz = Z // 2

    def ring(n, *inner):
        return [pltpu.VMEM((*m, *inner, 16, HALF), BF16) for m in ((n // 2,), (n // 2,), (2, n))]

    outs = pl.pallas_call(
        functools.partial(kernel, Z, inverse),
        out_shape=(
            jax.ShapeDtypeStruct((rows, 2 * HALF), BF16),
            jax.ShapeDtypeStruct((rows, D), BF16),
            jax.ShapeDtypeStruct((8, 2 * HALF), F32),
            jax.ShapeDtypeStruct((2 * Z, 128), F32),
        ),
        in_specs=[pl.BlockSpec(memory_space=pltpu.SMEM)] + [hbm] * 5,
        out_specs=(hbm,) * 4,
        scratch_shapes=[
            pltpu.VMEM((rows, D), BF16),
            pltpu.VMEM((rows, 2 * HALF), BF16),
            pltpu.VMEM(w_codes.shape, BF16),
            pltpu.VMEM(w_scales.shape, BF16),
            pltpu.VMEM((D // 128, 128), F32),
            pltpu.VMEM((rows, 2 * HALF), BF16),
            pltpu.VMEM((rows, D), BF16),
            pltpu.VMEM((8, 2 * HALF), F32),
            pltpu.VMEM((2 * Z, 128), F32),
            pltpu.VMEM((2, 8, HALF), F32),
            pltpu.VMEM((2, Z, 2, 4, 2, 16, HALF), BF16),
            pltpu.VMEM((rows, 2 * HALF), BF16),
            pltpu.VMEM((2, Z, 2, 4, 2, 16, HALF), BF16),
            pltpu.VMEM((Z, 2, 4, 2, 16, HALF), BF16),
            pltpu.VMEM((16, HALF), F32),
            pltpu.VMEM((8, HALF), F32),
            *ring(hz, 2, 2),
            *ring(hz, 4),
            pltpu.VMEM((hz, 2, 2, 16, HALF), BF16),
            pltpu.VMEM((hz, 4, 16, HALF), BF16),
            *ring(hz),
            *ring(hz),
            pltpu.VMEM((Z, 16, HALF), BF16),
            pltpu.VMEM((Z, 16, HALF), BF16),
            pltpu.VMEM((2, 8, HALF), F32),
            pltpu.VMEM((8, HALF), F32),
            pltpu.VMEM((1, Z * 16), F32),
            pltpu.VMEM((Z, 1, Z * 16), F32),
            pltpu.VMEM((Z, 128), F32),
            pltpu.VMEM((4, Z, 128), F32),
            pltpu.VMEM((Z, 128), F32),
            pltpu.VMEM((8, Z, 128), F32),
            dma((6,)),
            dma((4,)),
            dma((12,)),
            dma((12,)),
            dma((D // WIDE,)),
            dma((16,)), dma((8,)),
        ],
        compiler_params=pltpu.CompilerParams(
            collective_id=0, has_side_effects=True, vmem_limit_bytes=VMEM_BYTES
        ),
    )(seq_counts, tokens, key_grad, w_codes, w_scales, gain.reshape(D // 128, 128))
    keys, tig, wg, gg = pl.pallas_call(
        keep,
        out_shape=tuple(jax.ShapeDtypeStruct(o.shape, o.dtype) for o in outs),
        in_specs=[hbm] * 4,
        out_specs=(hbm,) * 4,
        scratch_shapes=[pltpu.VMEM(o.shape, o.dtype) for o in outs] + [dma((7,)), dma((7,))],
        compiler_params=pltpu.CompilerParams(vmem_limit_bytes=VMEM_BYTES),
    )(*outs)
    return keys, tig, wg, gg.reshape(D)


def solution(mesh):
    return jax.shard_map(
        local,
        mesh=mesh,
        in_specs=(
            P(("node", "local"), None),
            P(),
            P(None, ("node", "local"), None),
            P(None, ("node", "local")),
            P(("node", "local")),
            P(("node", "local"), None),
        ),
        out_specs=(
            P(("node", "local"), None),
            P(("node", "local"), None),
            P(("node", "local"), None),
            P(),
        ),
        check_vma=False,
    )
```

time: 79 us -> 62.2 us (0.79)
  Pallas kernels: 69.6 us -> 60.7 us
  local copies, waits for them, and re-layouts: 7.87 us -> 0 us
    pallas_call x1, Pallas kernels: 69.6 us -> 58.1 us  [local(): pl.pallas_call(functools.partial(kernel, Z, inverse), out_shape=(jax.Shap...]
    unnamed x13 -> x0, local copies, waits for them, and re-layouts: 7.25 us -> none
    pallas_call x0 -> x1, Pallas kernels: none -> 2.59 us  [local(): pl.pallas_call(keep, out_shape=tuple((jax.ShapeDtypeStruct(o.shape, o.dty...]
where the time goes in v3:
time: 62.2 us; the launch traced here: 62 us
  Pallas kernels  60.7 us (98%)
  between operations  1.29 us (2%)
    pallas_call x1, Pallas kernels, local(): pl.pallas_call(functools.partial(kernel, Z, inverse), out_shape=(jax.Shap...  58.1 us
    pallas_call x1, Pallas kernels, local(): pl.pallas_call(keep, out_shape=tuple((jax.ShapeDtypeStruct(o.shape, o.dty...  2.59 us

profile of v3, /device:TPU:1, one launch (start us, length us, event | category | flops | bytes accessed | tf_op | source)
XLA Modules:
  0.0 62.0 jit_solution(13438583536107960802)
XLA Ops:
  1.3 58.1 %shard_map.93 = (bf16[256,512]{1,0:T(8,128)(2,1)}, bf16[256,4096]{1,0:T(8,128)(2,1)}, f32[8,512]{1,0:T(8,128)}, f32[32,128]{1,0:T(8,128)}) custom-call(s32[1]{0:T(128)S(6)} %copy.10.cnt, bf16[256,4096]{1,0:T(8,128)(2,1)} %tok_hbm.1, bf16[256,512]{1,0:T(8,128)(2,1)} %kg_hbm.1, bf16[4,8,128]{2,1,0:T(8,128)(2,1)} %codes_hbm.1, bf16[4,8]{1,0:T(4,128)(2,1)} %scales_hbm.1, ...), custom_call_target="tpu_custom_call" | custom-call | tf_op jit(solution)/shard_map/pallas_call | solution.py:487
  59.4 2.6 %shard_map.94 = (bf16[256,512]{1,0:T(8,128)(2,1)}, bf16[256,4096]{1,0:T(8,128)(2,1)}, f32[8,512]{1,0:T(8,128)}, f32[32,128]{1,0:T(8,128)}) custom-call(bf16[256,512]{1,0:T(8,128)(2,1)} %get-tuple-element.12.keys, bf16[256,4096]{1,0:T(8,128)(2,1)} %get-tuple-element.13.tig, f32[8,512]{1,0:T(8,128)} %get-tuple-element.14.wg, f32[32,128]{1,0:T(8,128)} %get-tuple-element.15.gg), custom_call_target="tpu_custom_call" | custom-call | tf_op jit(solution)/shard_map/pallas_call | solution.py:541

commit v4 on v3

--- a/solution.py
+++ b/solution.py
@@ -10,7 +10,6 @@
 
 SEQ_LEN = 64
 HALF = 256
-TILE = 512
 WIDE = 1024
 MESH = pl.DeviceIdType.MESH
 F32 = jnp.float32
@@ -98,16 +97,20 @@
             block = ref.at[at(o, part)]
             return copy(block, block, self.send, self.recv.at[i], dev)
 
-        self.sends = (one(0, 0, whole, plus), one(1, 0, whole, minus), one(2, 3, near, plus), one(2, 1, far, minus))
-        self.recvs = (one(0, 3, whole, plus), one(1, 1, whole, minus))
+        self.first = (one(0, 0, near, plus), one(1, 0, far, minus), one(3, 0, far, plus), one(3, 0, near, minus))
+        self.relay = (one(2, 3, near, plus), one(2, 1, far, minus))
+        self.recvs = (one(0, 3, near, plus), one(1, 1, far, minus))
 
     def start(self):
-        self.sends[0].start()
-        self.sends[1].start()
+        for d in self.first:
+            d.start()
 
     def pass_on(self, i):
         self.recvs[i].wait_recv()
-        self.sends[2 + i].start()
+        self.relay[i].start()
+
+    def neighbours(self):
+        settle(self.opposite, recv=self.recv.at[3], dev=self.dev)
 
     def finish(self):
         settle(self.opposite, recv=self.recv.at[2], dev=self.dev)
@@ -116,19 +119,61 @@
         settle(like, send=self.send, dev=self.dev)
 
 
+class Sum:
+    def __init__(self, ref, at, n, got, sems, devs):
+        self.ref, self.at, self.n, self.got = ref, at, n, got
+        self.send, self.recv, self.dev = *sems, devs[1]
+        self.copies = [
+            copy(ref.at[at(o, pl.ds(0, n))], got.at[o - 1], self.send, self.recv, devs[o]) for o in (2, 1, 3)
+        ]
+
+    def start(self):
+        for d in self.copies:
+            d.start()
+
+    def finish(self, dst, dst_first):
+        settle(self.got, recv=self.recv, dev=self.dev)
+
+        def body(k, carry):
+            total = self.ref[self.at(0, k)].astype(F32)
+            for o in range(3):
+                total += self.got[o, k].astype(F32)
+            dst[dst_first + k] = total.astype(BF16)
+            return carry
+
+        lax.fori_loop(0, self.n, body, 0)
+
+    def sent(self):
+        settle(self.got, send=self.send, dev=self.dev)
+
+
+class Gather:
+    def __init__(self, block, sems, devs):
+        self.send, self.recv, self.dev = *sems, devs[1]
+        self.copies = [copy(block, block, self.send, self.recv, devs[o]) for o in (2, 1, 3)]
+
+    def start(self):
+        for d in self.copies:
+            d.start()
+
+    def finish(self, like):
+        settle(like, recv=self.recv, dev=self.dev)
+
+    def sent(self, like):
+        settle(like, send=self.send, dev=self.dev)
+
+
 def kernel(
     Z, inverse,
-    cnt, tok_hbm, kg_hbm, codes_hbm, scales_hbm, gain_hbm,
+    cnt_hbm, tok_hbm, kg_hbm, codes_hbm, scales_hbm, gain_hbm,
     keys_hbm, tig_hbm, wg_hbm, gg_hbm,
-    tok, kg, codes, scales, gain, keys, tig, wg, gg, wsh, W, M, G, GR, W16, wrecv,
+    cnt, tok, kg, codes, scales, gain, keys, tig, wg, gg, wsh, W, M, G, GR, W16, wrecv,
     ya, yb, ylr, xa, xb, xlr, Sy, Sx,
-    ya2, yb2, ylr2, xa2, xb2, xlr2, S3, zr, S4, wgr,
+    y2, x2, S3, zr, S4, wgr,
     qs, qz, qy, qyr, qx, qxr,
     in_s, out_s, ag_r, rs_r, cr_r, ms_s, ms_r,
 ):
     rows, D = tok.shape
-    tiles = D // TILE
-    zt = Z // tiles
     gtiles = D // WIDE
     gt = Z // gtiles
     hz = Z // 2
@@ -142,6 +187,10 @@
     def at_z(o):
         return (((z + o) % Z) * 2 + xlo, loc)
 
+    def far_first(i):
+        k = (i + 1) // 2
+        return Z // 2 + k - 2 * k * (i % 2)
+
     def at_y(o):
         return (node, ((y + o) % 4) * 4 + xhi * 2 + c)
 
@@ -154,12 +203,13 @@
     xs = [((x + o) % 4) % 2 for o in range(4)]
     xh = [((x + o) % 4) // 2 for o in range(4)]
 
-    loads = []
-    for i in range(2):
-        part = pl.ds(i * (D // 2), D // 2)
-        loads.append(pltpu.make_async_copy(tok_hbm.at[:, part], tok.at[:, part], in_s.at[i]))
-    for i, (a, b) in enumerate(((kg_hbm, kg), (codes_hbm, codes), (scales_hbm, scales), (gain_hbm, gain))):
-        loads.append(pltpu.make_async_copy(a, b, in_s.at[2 + i]))
+    small = ((codes_hbm, codes), (scales_hbm, scales), (gain_hbm, gain), (cnt_hbm, cnt))
+    loads = [pltpu.make_async_copy(a, b, in_s.at[i]) for i, (a, b) in enumerate(small)]
+    quarter = D // 4
+    for i in range(4):
+        part = pl.ds(i * quarter, quarter)
+        loads.append(pltpu.make_async_copy(tok_hbm.at[:, part], tok.at[:, part], in_s.at[4 + i]))
+    loads.append(pltpu.make_async_copy(kg_hbm, kg, in_s.at[8]))
     for d in loads:
         d.start()
 
@@ -173,13 +223,13 @@
         return carry
 
     greet(at_core)
-    lax.fori_loop(1, Z, hello, 0)
     for o in (1, 2, 3):
         greet(at_y(o))
         greet(at_x(o, c))
         greet(at_x(o, sib))
-
-    for d in loads[3:]:
+    lax.fori_loop(1, Z, hello, 0)
+
+    for d in loads[:3]:
         d.wait()
     chip = (node * 16 + loc) // 2
     lane = lax.broadcasted_iota(jnp.int32, (16, 128), 1)
@@ -192,23 +242,19 @@
         col = jnp.sum(jnp.where(eye, sc[b:b + 1, :], 0.0), axis=1, keepdims=True)
         wsh[b // 2, :, (b % 2) * 128:(b % 2 + 1) * 128] = codes[b].astype(F32) * col
 
-    def square(k, acc):
-        for i in range(TILE // 128):
-            t = tok[:, pl.ds(pl.multiple_of(k * TILE + i * 128, 128), 128)].astype(F32)
-            acc += t * t
-        return acc
-
-    loads[0].wait()
-    total = lax.fori_loop(0, tiles // 2, square, jnp.zeros((rows, 128), F32))
-    loads[1].wait()
-    total = lax.fori_loop(tiles // 2, tiles, square, total)
-    pl.semaphore_wait(barrier, Z - 1 + 10)
-    wx = copy(wsh.at[sib], wrecv, ms_s.at[1], ms_r.at[0], at_core)
-    wx.start()
-
+    total = jnp.zeros((rows, 128), F32)
+    for i in range(4):
+        loads[4 + i].wait()
+
+        def square(k, acc):
+            t = tok[:, pl.ds(pl.multiple_of(i * quarter + k * 128, 128), 128)].astype(F32)
+            return acc + t * t
+
+        total = lax.fori_loop(0, quarter // 128, square, total, unroll=True)
     rs = lax.rsqrt(jnp.sum(total, axis=1, keepdims=True) / D + 1e-05)
-    live = lax.broadcasted_iota(jnp.int32, (rows, 1), 0) // SEQ_LEN < cnt[0]
-    loads[2].wait()
+    loads[3].wait()
+    loads[8].wait()
+    live = lax.broadcasted_iota(jnp.int32, (rows, 1), 0) // SEQ_LEN < cnt[...]
     M[...] = (jnp.where(live, kg[...].astype(F32), 0.0) * rs).astype(BF16)
 
     def core_copy(k):
@@ -220,10 +266,19 @@
         g = lax.dot_general(t, M[...], (((0,), (0,)), ((), ())), preferred_element_type=F32).astype(BF16)
         for h in range(2):
             G[h, pl.ds(k * gt, gt)] = g[:, h * HALF:(h + 1) * HALF].reshape(gt, 2, 4, 2, 16, HALF)
+        return carry
+
+    def core_start(k, carry):
         core_copy(k).start()
         return carry
 
     lax.fori_loop(0, gtiles // 2, grad, 0)
+    pl.semaphore_wait(barrier, Z - 1 + 10)
+    wx = copy(wsh.at[sib], wrecv, ms_s.at[1], ms_r.at[0], at_core)
+    wx.start()
+    lax.fori_loop(0, gtiles // 2, core_start, 0)
+    lax.fori_loop(gtiles // 2, gtiles, grad, 0)
+    lax.fori_loop(gtiles // 2, gtiles, core_start, 0)
 
     wx.wait_recv()
     own, other = wsh[c], wrecv[...]
@@ -235,13 +290,11 @@
         block = W.at[c, src_z, xlo, y, xhi]
         return copy(block, block, ms_s.at[2], ms_r.at[1], at_z(o))
 
-    def agz_start(o, carry):
-        agz(o, z).start()
-        return carry
-
-    lax.fori_loop(1, Z, agz_start, 0)
-
-    lax.fori_loop(gtiles // 2, gtiles, grad, 0)
+    def agz_start(i, carry):
+        agz(far_first(i), z).start()
+        return carry
+
+    lax.fori_loop(0, Z - 1, agz_start, 0)
 
     def core_add(k, carry):
         core_copy(k).wait_recv()
@@ -252,28 +305,35 @@
     def sems(i, pair, j, n):
         return ms_s.at[i], pair.at[pl.ds(j, n)]
 
-    sum_y = RingSum(G, lambda o, p: (c, p, ALL, ys[o]), 0, hz, (ya, yb, ylr), sems(8, rs_r, 0, 3), at_y(1), at_y(3))
+    devs_y = [at_y(o) for o in range(4)]
+    devs_x = [at_x(o, c) for o in range(4)]
+    low, high = pl.ds(0, hz), pl.ds(hz, hz)
+    sum_y = RingSum(
+        G, lambda o, p: (c, p, ALL, ys[o]), 0, hz, (ya, yb, ylr), sems(8, rs_r, 0, 3), devs_y[1], devs_y[3]
+    )
     sum_x = RingSum(
-        G, lambda o, p: (c, p, xs[o], ALL, xh[o]), hz, hz, (xa, xb, xlr), sems(9, rs_r, 3, 3), at_x(1, c), at_x(3, c)
+        G, lambda o, p: (c, p, xs[o], ALL, xh[o]), hz, hz, (xa, xb, xlr), sems(9, rs_r, 3, 3), devs_x[1], devs_x[3]
     )
-    sum_yx = RingSum(
-        Sy, lambda o, p: (p, xs[o], xh[o]), 0, hz, (xa2, xb2, xlr2), sems(10, rs_r, 6, 3), at_x(1, c), at_x(3, c)
+    sum_yx = Sum(Sy, lambda o, p: (p, xs[o], xh[o]), hz, x2, (ms_s.at[10], rs_r.at[6]), devs_x)
+    sum_xy = Sum(Sx, lambda o, p: (p, ys[o]), hz, y2, (ms_s.at[11], rs_r.at[7]), devs_y)
+    get_y = Gather(W.at[c, low, xlo, y, xhi], (ms_s.at[12], rs_r.at[8]), devs_y)
+    get_x = Gather(W.at[c, high, xlo, y, xhi], (ms_s.at[13], rs_r.at[9]), devs_x)
+    get_yx = RingGather(
+        W, lambda o, p: (c, p, xs[o], ALL, xh[o]), 0, hz, sems(14, ag_r, 0, 4), devs_x[1], devs_x[3]
     )
-    sum_xy = RingSum(Sx, lambda o, p: (p, ys[o]), 0, hz, (ya2, yb2, ylr2), sems(11, rs_r, 9, 3), at_y(1), at_y(3))
-    get_y = RingGather(W, lambda o, p: (c, p, xlo, ys[o], xhi), 0, hz, sems(12, ag_r, 0, 3), at_y(1), at_y(3))
-    get_x = RingGather(W, lambda o, p: (c, p, xs[o], y, xh[o]), hz, hz, sems(13, ag_r, 3, 3), at_x(1, c), at_x(3, c))
-    get_yx = RingGather(
-        W, lambda o, p: (c, p, xs[o], ALL, xh[o]), 0, hz, sems(14, ag_r, 6, 3), at_x(1, c), at_x(3, c)
-    )
-    get_xy = RingGather(W, lambda o, p: (c, p, ALL, ys[o]), hz, hz, sems(15, ag_r, 9, 3), at_y(1), at_y(3))
-
-    def hand_yx(o, half):
-        block = W.at[half, pl.ds(0, hz), xs[o], :, xh[o]]
-        return copy(block, block, ms_s.at[3], ms_r.at[2], at_core)
-
-    def hand_xy(o, half):
-        block = W.at[half, pl.ds(hz, hz), :, ys[o]]
-        return copy(block, block, ms_s.at[3], ms_r.at[2], at_core)
+    get_xy = RingGather(W, lambda o, p: (c, p, ALL, ys[o]), hz, hz, sems(15, ag_r, 4, 4), devs_y[1], devs_y[3])
+    three = W.at[c, low, xlo, pl.ds(0, 3), xhi]
+
+    near, far = pl.ds(0, hz // 2), pl.ds(hz // 2, hz // 2)
+    near2, far2 = pl.ds(hz, hz // 2), pl.ds(hz + hz // 2, hz // 2)
+
+    def hand_yx(o, part):
+        block = W.at[c, part, xs[o], :, xh[o]]
+        copy(block, block, ms_s.at[3], ms_r.at[2], at_core).start()
+
+    def hand_xy(o, part):
+        block = W.at[c, part, :, ys[o]]
+        copy(block, block, ms_s.at[3], ms_r.at[2], at_core).start()
 
     lax.fori_loop(0, gtiles // 2, core_add, 0)
     sum_y.start()
@@ -290,17 +350,12 @@
     sum_yx.start()
     sum_x.finish(Sx, 0)
     sum_xy.start()
-    for i in range(2):
-        get_y.pass_on(i)
-        get_x.pass_on(i)
-    sum_yx.forward()
-    sum_xy.forward()
-    get_y.finish()
+    get_y.finish(three)
     get_yx.start()
-    hand_yx(0, c).start()
-    get_x.finish()
+    hand_yx(0, low)
+    get_x.finish(three)
     get_xy.start()
-    hand_xy(0, c).start()
+    hand_xy(0, high)
     sum_yx.finish(S3, 0)
     sum_xy.finish(S3, hz)
 
@@ -311,26 +366,27 @@
     def gqz(o, src_z):
         return copy(qs, qz.at[src_z], ms_s.at[5], ms_r.at[4], at_z(o))
 
-    def gqz_start(o, carry):
-        gqz(o, z).start()
-        return carry
-
-    lax.fori_loop(1, Z, gqz_start, 0)
+    def gqz_start(i, carry):
+        gqz(far_first(i), z).start()
+        return carry
+
+    lax.fori_loop(0, Z - 1, gqz_start, 0)
 
     def rsz(o, dst_z, src_z):
         return copy(S3.at[dst_z], zr.at[src_z], ms_s.at[4], ms_r.at[3], at_z(o))
 
-    def rsz_start(o, carry):
+    def rsz_start(i, carry):
+        o = far_first(i)
         rsz(o, (z + o) % Z, z).start()
         return carry
 
-    lax.fori_loop(1, Z, rsz_start, 0)
+    lax.fori_loop(0, Z - 1, rsz_start, 0)
 
     for i, o in ((0, 3), (1, 1)):
         get_yx.pass_on(i)
-        hand_yx(o, c).start()
+        hand_yx(o, (near, far)[i])
         get_xy.pass_on(i)
-        hand_xy(o, c).start()
+        hand_xy(o, (near2, far2)[i])
 
     def gqz_add(o, acc):
         src = (z + Z - o) % Z
@@ -349,11 +405,34 @@
     for d in qys:
         d.start()
 
+    get_yx.neighbours()
+    hand_yx(3, far)
+    hand_yx(1, near)
+    get_xy.neighbours()
+    hand_xy(3, far2)
+    hand_xy(1, near2)
     get_yx.finish()
-    hand_yx(2, c).start()
+    hand_yx(2, low)
     get_xy.finish()
-    hand_xy(2, c).start()
-
+    hand_xy(2, high)
+
+    span = D // 2
+
+    def project(h):
+        def body(k, acc):
+            t = tok[:, pl.ds(pl.multiple_of(k * span, span), span)]
+            w = W[h, pl.ds(k * hz, hz)].reshape(span, HALF)
+            return acc + jnp.dot(t, w, preferred_element_type=F32)
+
+        prod = lax.fori_loop(0, 2, body, jnp.zeros((rows, HALF), F32))
+        kf = jnp.where(live, prod * rs, 0.0)
+        cols = pl.ds(pl.multiple_of(h * HALF, HALF), HALF)
+        keys[:, cols] = kf.astype(BF16)
+        return jnp.sum(kf * kg[:, cols].astype(F32), axis=1, keepdims=True)
+
+    mean = project(c)
+
+    settle(W.at[sib], recv=ms_r.at[2], dev=at_core)
     settle(qyr.at[pl.ds(0, 3)], recv=ms_r.at[6], dev=at_core)
     qx[...] = qy[...] + qyr[1] + qyr[2] + qyr[3]
     qxs = [
@@ -363,36 +442,7 @@
     for d in qxs:
         d.start()
 
-    def rsz_add(o, acc):
-        src = (z + Z - o) % Z
-        return acc + zr[src].astype(F32)
-
-    settle(zr.at[pl.ds(0, Z - 1)], recv=ms_r.at[3], dev=at_core)
-    s4 = lax.fori_loop(1, Z, rsz_add, S3[z].astype(F32))
-
-    s4 = s4 * (g16 * inverse)
-    S4[0] = s4[0:8]
-    S4[1] = s4[8:16]
-    gx = copy(S4.at[sib], wgr, ms_s.at[1], ms_r.at[5], at_core)
-    gx.start()
-
-    settle(W.at[sib], recv=ms_r.at[2], dev=at_core)
-    span = D // 2
-
-    def project(k, acc):
-        t = tok[:, pl.ds(pl.multiple_of(k * span, span), span)]
-        return tuple(
-            acc[h] + jnp.dot(t, W[h, pl.ds(k * hz, hz)].reshape(span, HALF), preferred_element_type=F32)
-            for h in range(2)
-        )
-
-    zero = jnp.zeros((rows, HALF), F32)
-    prods = lax.fori_loop(0, 2, project, (zero, zero))
-    mean = jnp.zeros((rows, 1), F32)
-    for h in range(2):
-        kf = jnp.where(live, prods[h] * rs, 0.0)
-        keys[:, h * HALF:(h + 1) * HALF] = kf.astype(BF16)
-        mean += jnp.sum(kf * kg[:, h * HALF:(h + 1) * HALF].astype(F32), axis=1, keepdims=True)
+    mean += project(sib)
     coef = rs * rs * (mean / D)
     stores = [
         pltpu.make_async_copy(a, b, out_s.at[i])
@@ -400,19 +450,32 @@
     ]
     stores[0].start()
 
+    def rsz_add(o, acc):
+        src = (z + Z - o) % Z
+        return acc + zr[src].astype(F32)
+
+    settle(zr.at[pl.ds(0, Z - 1)], recv=ms_r.at[3], dev=at_core)
+    s4 = lax.fori_loop(1, Z, rsz_add, S3[z].astype(F32))
+
+    s4 = s4 * (g16 * inverse)
+    S4[0] = s4[0:8]
+    S4[1] = s4[8:16]
+    gx = copy(S4.at[sib], wgr, ms_s.at[1], ms_r.at[5], at_core)
+    gx.start()
+
     def back(k, carry):
-        cols = pl.ds(pl.multiple_of(k * TILE, TILE), TILE)
+        cols = pl.ds(pl.multiple_of(k * WIDE, WIDE), WIDE)
         d = -(tok[:, cols].astype(F32) * coef)
         for h in range(2):
             d += lax.dot_general(
-                M[:, h * HALF:(h + 1) * HALF], W[h, pl.ds(k * zt, zt)].reshape(TILE, HALF),
+                M[:, h * HALF:(h + 1) * HALF], W[h, pl.ds(k * gt, gt)].reshape(WIDE, HALF),
                 (((1,), (1,)), ((), ())), preferred_element_type=F32,
             )
         tig[:, cols] = d.astype(BF16)
         pltpu.make_async_copy(tig.at[:, cols], tig_hbm.at[:, cols], out_s.at[3]).start()
         return carry
 
-    lax.fori_loop(0, tiles, back, 0)
+    lax.fori_loop(0, gtiles, back, 0)
 
     gx.wait_recv()
     own, other = S4[c], wgr[...]
@@ -443,10 +506,10 @@
         settle(ref, send=ms_s.at[i], dev=at_core)
     sum_y.sent(G.at[c, pl.ds(0, hz), :, pl.ds(0, 3)])
     sum_x.sent(G.at[c, pl.ds(0, hz), :, pl.ds(0, 3)])
-    sum_yx.sent(Sx.at[:, pl.ds(0, 3)])
-    sum_xy.sent(Sx.at[:, pl.ds(0, 3)])
-    get_y.sent(W.at[c, pl.ds(0, hz), xlo, pl.ds(0, 3), xhi])
-    get_x.sent(W.at[c, pl.ds(0, hz), xlo, pl.ds(0, 3), xhi])
+    sum_yx.sent()
+    sum_xy.sent()
+    get_y.sent(three)
+    get_x.sent(three)
     get_yx.sent(W.at[c, pl.ds(0, hz), :, pl.ds(0, 3)])
     get_xy.sent(W.at[c, pl.ds(0, hz), :, pl.ds(0, 3)])
     pltpu.make_async_copy(tig, tig_hbm, out_s.at[3]).wait()
@@ -492,9 +555,10 @@
             jax.ShapeDtypeStruct((8, 2 * HALF), F32),
             jax.ShapeDtypeStruct((2 * Z, 128), F32),
         ),
-        in_specs=[pl.BlockSpec(memory_space=pltpu.SMEM)] + [hbm] * 5,
+        in_specs=[hbm] * 6,
         out_specs=(hbm,) * 4,
         scratch_shapes=[
+            pltpu.VMEM((1, 1), jnp.int32),
             pltpu.VMEM((rows, D), BF16),
             pltpu.VMEM((rows, 2 * HALF), BF16),
             pltpu.VMEM(w_codes.shape, BF16),
@@ -515,8 +579,8 @@
             *ring(hz, 4),
             pltpu.VMEM((hz, 2, 2, 16, HALF), BF16),
             pltpu.VMEM((hz, 4, 16, HALF), BF16),
-            *ring(hz),
-            *ring(hz),
+            pltpu.VMEM((3, hz, 16, HALF), BF16),
+            pltpu.VMEM((3, hz, 16, HALF), BF16),
             pltpu.VMEM((Z, 16, HALF), BF16),
             pltpu.VMEM((Z, 16, HALF), BF16),
             pltpu.VMEM((2, 8, HALF), F32),
@@ -527,17 +591,17 @@
             pltpu.VMEM((4, Z, 128), F32),
             pltpu.VMEM((Z, 128), F32),
             pltpu.VMEM((8, Z, 128), F32),
-            dma((6,)),
+            dma((9,)),
             dma((4,)),
-            dma((12,)),
-            dma((12,)),
+            dma((8,)),
+            dma((10,)),
             dma((D // WIDE,)),
             dma((16,)), dma((8,)),
         ],
         compiler_params=pltpu.CompilerParams(
             collective_id=0, has_side_effects=True, vmem_limit_bytes=VMEM_BYTES
         ),
-    )(seq_counts, tokens, key_grad, w_codes, w_scales, gain.reshape(D // 128, 128))
+    )(seq_counts.reshape(1, 1), tokens, key_grad, w_codes, w_scales, gain.reshape(D // 128, 128))
     keys, tig, wg, gg = pl.pallas_call(
         keep,
         out_shape=tuple(jax.ShapeDtypeStruct(o.shape, o.dtype) for o in outs),

time: 62.2 us -> 58.9 us (0.947)
  Pallas kernels: 60.7 us -> 57.4 us
    pallas_call x1, Pallas kernels: 58.1 us -> 54.8 us  [local(): pl.pallas_call(functools.partial(kernel, Z, inverse), out_shape=(jax.Shap...]
where the time goes in v4:
time: 58.9 us; the launch traced here: 58.7 us
  Pallas kernels  57.4 us (97%)
  between operations  1.29 us (2%)
    pallas_call x1, Pallas kernels, local(): pl.pallas_call(functools.partial(kernel, Z, inverse), out_shape=(jax.Shap...  54.8 us
    pallas_call x1, Pallas kernels, local(): pl.pallas_call(keep, out_shape=tuple((jax.ShapeDtypeStruct(o.shape, o.dty...  2.59 us

profile of v4, /device:TPU:1, one launch (start us, length us, event | category | flops | bytes accessed | tf_op | source)
XLA Modules:
  0.0 58.7 jit_solution(6867469922942512314)
XLA Ops:
  1.3 54.8 %shard_map.93 = (bf16[256,512]{1,0:T(8,128)(2,1)}, bf16[256,4096]{1,0:T(8,128)(2,1)}, f32[8,512]{1,0:T(8,128)}, f32[32,128]{1,0:T(8,128)}) custom-call(s32[1,1]{1,0:T(1,128)} %bitcast.3.cnt_hbm, bf16[256,4096]{1,0:T(8,128)(2,1)} %tok_hbm.1, bf16[256,512]{1,0:T(8,128)(2,1)} %kg_hbm.1, bf16[4,8,128]{2,1,0:T(8,128)(2,1)} %codes_hbm.1, bf16[4,8]{1,0:T(4,128)(2,1)} %scales_hbm.1, ...), custom_call_target="tpu_custom_call" | custom-call | tf_op jit(solution)/shard_map/pallas_call | solution.py:550
  56.1 2.6 %shard_map.94 = (bf16[256,512]{1,0:T(8,128)(2,1)}, bf16[256,4096]{1,0:T(8,128)(2,1)}, f32[8,512]{1,0:T(8,128)}, f32[32,128]{1,0:T(8,128)}) custom-call(bf16[256,512]{1,0:T(8,128)(2,1)} %get-tuple-element.12.keys, bf16[256,4096]{1,0:T(8,128)(2,1)} %get-tuple-element.13.tig, f32[8,512]{1,0:T(8,128)} %get-tuple-element.14.wg, f32[32,128]{1,0:T(8,128)} %get-tuple-element.15.gg), custom_call_target="tpu_custom_call" | custom-call | tf_op jit(solution)/shard_map/pallas_call | solution.py:605

commit v5 on v4

--- a/solution.py
+++ b/solution.py
@@ -167,11 +167,11 @@
     Z, inverse,
     cnt_hbm, tok_hbm, kg_hbm, codes_hbm, scales_hbm, gain_hbm,
     keys_hbm, tig_hbm, wg_hbm, gg_hbm,
-    cnt, tok, kg, codes, scales, gain, keys, tig, wg, gg, wsh, W, M, G, GR, W16, wrecv,
+    cnt, tok, kg, codes, scales, gain, keys, tig, wg, gg, wsh, W, M, G, GR, W16, wrecv, wother,
     ya, yb, ylr, xa, xb, xlr, Sy, Sx,
     y2, x2, S3, zr, S4, wgr,
     qs, qz, qy, qyr, qx, qxr,
-    in_s, out_s, ag_r, rs_r, cr_r, ms_s, ms_r,
+    met, in_s, out_s, ag_r, rs_r, cr_r, ms_s, ms_r,
 ):
     rows, D = tok.shape
     gtiles = D // WIDE
@@ -218,16 +218,18 @@
     def greet(dev):
         pl.semaphore_signal(barrier, inc=1, device_id=dev, device_id_type=MESH)
 
-    def hello(o, carry):
-        greet(at_z(o))
+    def hello(i, carry):
+        greet((((z + far_first(i)) % Z) * 2 + xlo, y * 4 + xhi * 2 + 1))
         return carry
 
-    greet(at_core)
+    lax.fori_loop(0, Z - 1, hello, 0)
     for o in (1, 2, 3):
-        greet(at_y(o))
-        greet(at_x(o, c))
-        greet(at_x(o, sib))
-    lax.fori_loop(1, Z, hello, 0)
+        greet((node, ((y + o) % 4) * 4 + xhi * 2))
+        greet(at_x(o, 0))
+
+    @pl.when(c == 1)
+    def _():
+        greet(at_core)
 
     for d in loads[:3]:
         d.wait()
@@ -273,28 +275,52 @@
         return carry
 
     lax.fori_loop(0, gtiles // 2, grad, 0)
-    pl.semaphore_wait(barrier, Z - 1 + 10)
-    wx = copy(wsh.at[sib], wrecv, ms_s.at[1], ms_r.at[0], at_core)
+
+    @pl.when(c == 0)
+    def _():
+        pl.semaphore_wait(barrier, 13)
+        pl.semaphore_signal(met.at[0], inc=1, device_id=at_core, device_id_type=MESH)
+
+    @pl.when(c == 1)
+    def _():
+        pl.semaphore_wait(met.at[0], 1)
+
+    wx = copy(wsh, wrecv, ms_s.at[1], ms_r.at[0], at_core)
     wx.start()
     lax.fori_loop(0, gtiles // 2, core_start, 0)
     lax.fori_loop(gtiles // 2, gtiles, grad, 0)
     lax.fori_loop(gtiles // 2, gtiles, core_start, 0)
 
     wx.wait_recv()
-    own, other = wsh[c], wrecv[...]
-    W16[0:8, :] = jnp.where(c == 0, own, other)
-    W16[8:16, :] = jnp.where(c == 0, other, own)
-    W[c, z, xlo, y, xhi] = (W16[...] * g16).astype(BF16)
-
-    def agz(o, src_z):
-        block = W.at[c, src_z, xlo, y, xhi]
-        return copy(block, block, ms_s.at[2], ms_r.at[1], at_z(o))
-
-    def agz_start(i, carry):
-        agz(far_first(i), z).start()
-        return carry
-
-    lax.fori_loop(0, Z - 1, agz_start, 0)
+
+    def rows16(h):
+        own, other = wsh[h], wrecv[h]
+        W16[0:8, :] = jnp.where(c == 0, own, other)
+        W16[8:16, :] = jnp.where(c == 0, other, own)
+        return (W16[...] * g16).astype(BF16)
+
+    W[c, z, xlo, y, xhi] = rows16(c)
+
+    def agz(o):
+        zz = (z + o) % Z
+        place = (z, xlo, y, xhi)
+        return tuple(
+            copy(src, W.at[h, *place], ms_s.at[2], ms_r.at[1], (zz * 2 + xlo, y * 4 + xhi * 2 + h))
+            for h, src in ((1, W.at[1, *place]), (0, wother))
+        )
+
+    @pl.when(c == 1)
+    def _():
+        wother[...] = rows16(0)
+        pl.semaphore_wait(barrier, 2 * (Z - 1))
+        pl.semaphore_signal(met.at[1], inc=1, device_id=at_core, device_id_type=MESH)
+
+        def agz_start(i, carry):
+            for d in agz(far_first(i)):
+                d.start()
+            return carry
+
+        lax.fori_loop(0, Z - 1, agz_start, 0)
 
     def core_add(k, carry):
         core_copy(k).wait_recv()
@@ -343,35 +369,39 @@
     sum_y.forward()
     sum_x.forward()
 
-    settle(W.at[c, pl.ds(0, Z - 1), xlo, y, xhi], recv=ms_r.at[1], dev=at_core)
-    get_y.start()
-    get_x.start()
     sum_y.finish(Sy, 0)
     sum_yx.start()
     sum_x.finish(Sx, 0)
     sum_xy.start()
+    settle(W.at[c, pl.ds(0, Z - 1), xlo, y, xhi], recv=ms_r.at[1], dev=at_core)
+    get_y.start()
+    get_x.start()
+    sum_yx.finish(S3, 0)
+    sum_xy.finish(S3, hz)
+
+    q = jnp.sum(W[c, :, xlo, y, xhi].astype(F32) * S3[...].astype(F32), axis=2, keepdims=True).reshape(Z * 16, 1)
+    diag = lax.broadcasted_iota(jnp.int32, (Z * 16, Z * 16), 0) == lax.broadcasted_iota(jnp.int32, (Z * 16, Z * 16), 1)
+    qs[...] = jnp.sum(jnp.where(diag, q, 0.0), axis=0, keepdims=True)
+
+    def gqz(o, src_z):
+        return copy(qs, qz.at[src_z], ms_s.at[5], ms_r.at[4], at_z(o))
+
+    def gqz_start(i, carry):
+        gqz(far_first(i), z).start()
+        return carry
+
+    @pl.when(c == 0)
+    def _():
+        pl.semaphore_wait(met.at[1], 1)
+
+    lax.fori_loop(0, Z - 1, gqz_start, 0)
+
     get_y.finish(three)
     get_yx.start()
     hand_yx(0, low)
     get_x.finish(three)
     get_xy.start()
     hand_xy(0, high)
-    sum_yx.finish(S3, 0)
-    sum_xy.finish(S3, hz)
-
-    q = jnp.sum(W[c, :, xlo, y, xhi].astype(F32) * S3[...].astype(F32), axis=2, keepdims=True).reshape(Z * 16, 1)
-    diag = lax.broadcasted_iota(jnp.int32, (Z * 16, Z * 16), 0) == lax.broadcasted_iota(jnp.int32, (Z * 16, Z * 16), 1)
-    qs[...] = jnp.sum(jnp.where(diag, q, 0.0), axis=0, keepdims=True)
-
-    def gqz(o, src_z):
-        return copy(qs, qz.at[src_z], ms_s.at[5], ms_r.at[4], at_z(o))
-
-    def gqz_start(i, carry):
-        gqz(far_first(i), z).start()
-        return carry
-
-    lax.fori_loop(0, Z - 1, gqz_start, 0)
-
     def rsz(o, dst_z, src_z):
         return copy(S3.at[dst_z], zr.at[src_z], ms_s.at[4], ms_r.at[3], at_z(o))
 
@@ -387,6 +417,13 @@
         hand_yx(o, (near, far)[i])
         get_xy.pass_on(i)
         hand_xy(o, (near2, far2)[i])
+
+    get_yx.neighbours()
+    hand_yx(3, far)
+    hand_yx(1, near)
+    get_xy.neighbours()
+    hand_xy(3, far2)
+    hand_xy(1, near2)
 
     def gqz_add(o, acc):
         src = (z + Z - o) % Z
@@ -405,12 +442,6 @@
     for d in qys:
         d.start()
 
-    get_yx.neighbours()
-    hand_yx(3, far)
-    hand_yx(1, near)
-    get_xy.neighbours()
-    hand_xy(3, far2)
-    hand_xy(1, near2)
     get_yx.finish()
     hand_yx(2, low)
     get_xy.finish()
@@ -432,7 +463,6 @@
 
     mean = project(c)
 
-    settle(W.at[sib], recv=ms_r.at[2], dev=at_core)
     settle(qyr.at[pl.ds(0, 3)], recv=ms_r.at[6], dev=at_core)
     qx[...] = qy[...] + qyr[1] + qyr[2] + qyr[3]
     qxs = [
@@ -442,6 +472,20 @@
     for d in qxs:
         d.start()
 
+    def rsz_add(o, acc):
+        src = (z + Z - o) % Z
+        return acc + zr[src].astype(F32)
+
+    settle(zr.at[pl.ds(0, Z - 1)], recv=ms_r.at[3], dev=at_core)
+    s4 = lax.fori_loop(1, Z, rsz_add, S3[z].astype(F32))
+
+    s4 = s4 * (g16 * inverse)
+    S4[0] = s4[0:8]
+    S4[1] = s4[8:16]
+    gx = copy(S4.at[sib], wgr, ms_s.at[1], ms_r.at[5], at_core)
+    gx.start()
+
+    settle(W.at[sib], recv=ms_r.at[2], dev=at_core)
     mean += project(sib)
     coef = rs * rs * (mean / D)
     stores = [
@@ -449,19 +493,6 @@
         for i, (a, b) in enumerate(((keys, keys_hbm), (wg, wg_hbm), (gg, gg_hbm)))
     ]
     stores[0].start()
-
-    def rsz_add(o, acc):
-        src = (z + Z - o) % Z
-        return acc + zr[src].astype(F32)
-
-    settle(zr.at[pl.ds(0, Z - 1)], recv=ms_r.at[3], dev=at_core)
-    s4 = lax.fori_loop(1, Z, rsz_add, S3[z].astype(F32))
-
-    s4 = s4 * (g16 * inverse)
-    S4[0] = s4[0:8]
-    S4[1] = s4[8:16]
-    gx = copy(S4.at[sib], wgr, ms_s.at[1], ms_r.at[5], at_core)
-    gx.start()
 
     def back(k, carry):
         cols = pl.ds(pl.multiple_of(k * WIDE, WIDE), WIDE)
@@ -500,10 +531,15 @@
     wx.wait_send()
     gx.wait_send()
     for ref, i in (
-        (G.at[sib], 0), (W.at[c, pl.ds(0, Z - 1), xlo, y, xhi], 2), (W.at[c], 3), (S3.at[pl.ds(0, Z - 1)], 4),
+        (G.at[sib], 0), (W.at[c], 3), (S3.at[pl.ds(0, Z - 1)], 4),
         (qz.at[pl.ds(0, Z - 1)], 5), (qyr.at[pl.ds(0, 3)], 6), (qxr.at[pl.ds(0, 7)], 7),
     ):
         settle(ref, send=ms_s.at[i], dev=at_core)
+
+    @pl.when(c == 1)
+    def _():
+        settle(W.at[:, pl.ds(0, Z - 1), xlo, y, xhi], send=ms_s.at[2], dev=at_core)
+
     sum_y.sent(G.at[c, pl.ds(0, hz), :, pl.ds(0, 3)])
     sum_x.sent(G.at[c, pl.ds(0, hz), :, pl.ds(0, 3)])
     sum_yx.sent()
@@ -574,7 +610,8 @@
             pltpu.VMEM((2, Z, 2, 4, 2, 16, HALF), BF16),
             pltpu.VMEM((Z, 2, 4, 2, 16, HALF), BF16),
             pltpu.VMEM((16, HALF), F32),
-            pltpu.VMEM((8, HALF), F32),
+            pltpu.VMEM((2, 8, HALF), F32),
+            pltpu.VMEM((16, HALF), BF16),
             *ring(hz, 2, 2),
             *ring(hz, 4),
             pltpu.VMEM((hz, 2, 2, 16, HALF), BF16),
@@ -591,6 +628,7 @@
             pltpu.VMEM((4, Z, 128), F32),
             pltpu.VMEM((Z, 128), F32),
             pltpu.VMEM((8, Z, 128), F32),
+            pltpu.SemaphoreType.REGULAR((2,)),
             dma((9,)),
             dma((4,)),
             dma((8,)),

time: 58.9 us -> 57.1 us (0.969)
  Pallas kernels: 57.4 us -> 55.6 us
    pallas_call x1, Pallas kernels: 54.8 us -> 53 us  [local(): pl.pallas_call(functools.partial(kernel, Z, inverse), out_shape=(jax.Shap...]
where the time goes in v5:
time: 57.1 us; the launch traced here: 56.9 us
  Pallas kernels  55.6 us (97%)
  between operations  1.29 us (2%)
    pallas_call x1, Pallas kernels, local(): pl.pallas_call(functools.partial(kernel, Z, inverse), out_shape=(jax.Shap...  53 us
    pallas_call x1, Pallas kernels, local(): pl.pallas_call(keep, out_shape=tuple((jax.ShapeDtypeStruct(o.shape, o.dty...  2.59 us

profile of v5, /device:TPU:1, one launch (start us, length us, event | category | flops | bytes accessed | tf_op | source)
XLA Modules:
  0.0 56.9 jit_solution(16265164182726216940)
XLA Ops:
  1.3 53.0 %shard_map.93 = (bf16[256,512]{1,0:T(8,128)(2,1)}, bf16[256,4096]{1,0:T(8,128)(2,1)}, f32[8,512]{1,0:T(8,128)}, f32[32,128]{1,0:T(8,128)}) custom-call(s32[1,1]{1,0:T(1,128)} %bitcast.3.cnt_hbm, bf16[256,4096]{1,0:T(8,128)(2,1)} %tok_hbm.1, bf16[256,512]{1,0:T(8,128)(2,1)} %kg_hbm.1, bf16[4,8,128]{2,1,0:T(8,128)(2,1)} %codes_hbm.1, bf16[4,8]{1,0:T(4,128)(2,1)} %scales_hbm.1, ...), custom_call_target="tpu_custom_call" | custom-call | tf_op jit(solution)/shard_map/pallas_call | solution.py:586
  54.3 2.6 %shard_map.94 = (bf16[256,512]{1,0:T(8,128)(2,1)}, bf16[256,4096]{1,0:T(8,128)(2,1)}, f32[8,512]{1,0:T(8,128)}, f32[32,128]{1,0:T(8,128)}) custom-call(bf16[256,512]{1,0:T(8,128)(2,1)} %get-tuple-element.12.keys, bf16[256,4096]{1,0:T(8,128)(2,1)} %get-tuple-element.13.tig, f32[8,512]{1,0:T(8,128)} %get-tuple-element.14.wg, f32[32,128]{1,0:T(8,128)} %get-tuple-element.15.gg), custom_call_target="tpu_custom_call" | custom-call | tf_op jit(solution)/shard_map/pallas_call | solution.py:643

commit v6 on v5

--- a/solution.py
+++ b/solution.py
@@ -166,11 +166,11 @@
 def kernel(
     Z, inverse,
     cnt_hbm, tok_hbm, kg_hbm, codes_hbm, scales_hbm, gain_hbm,
-    keys_hbm, tig_hbm, wg_hbm, gg_hbm,
-    cnt, tok, kg, codes, scales, gain, keys, tig, wg, gg, wsh, W, M, G, GR, W16, wrecv, wother,
+    keys_hbm, tig_hbm, wg_hbm, qxr,
+    cnt, tok, kg, codes, scales, gain, keys, tig, wsh, W, M, G, GR, W16, wrecv, wother,
     ya, yb, ylr, xa, xb, xlr, Sy, Sx,
-    y2, x2, S3, zr, S4, wgr,
-    qs, qz, qy, qyr, qx, qxr,
+    y2, x2, S3, zr, S4,
+    qs, qz, qy, qyr, qx,
     met, in_s, out_s, ag_r, rs_r, cr_r, ms_s, ms_r,
 ):
     rows, D = tok.shape
@@ -256,7 +256,7 @@
     rs = lax.rsqrt(jnp.sum(total, axis=1, keepdims=True) / D + 1e-05)
     loads[3].wait()
     loads[8].wait()
-    live = lax.broadcasted_iota(jnp.int32, (rows, 1), 0) // SEQ_LEN < cnt[...]
+    live = lax.broadcasted_iota(jnp.int32, (rows, 1), 0) // SEQ_LEN < cnt[0]
     M[...] = (jnp.where(live, kg[...].astype(F32), 0.0) * rs).astype(BF16)
 
     def core_copy(k):
@@ -463,6 +463,7 @@
 
     mean = project(c)
 
+    settle(W.at[sib], recv=ms_r.at[2], dev=at_core)
     settle(qyr.at[pl.ds(0, 3)], recv=ms_r.at[6], dev=at_core)
     qx[...] = qy[...] + qyr[1] + qyr[2] + qyr[3]
     qxs = [
@@ -471,6 +472,13 @@
     ]
     for d in qxs:
         d.start()
+    qx_out = pltpu.make_async_copy(qx, qxr.at[0], out_s.at[0])
+    qx_out.start()
+
+    mean += project(sib)
+    coef = rs * rs * (mean / D)
+    keys_out = pltpu.make_async_copy(keys, keys_hbm, out_s.at[2])
+    keys_out.start()
 
     def rsz_add(o, acc):
         src = (z + Z - o) % Z
@@ -482,17 +490,11 @@
     s4 = s4 * (g16 * inverse)
     S4[0] = s4[0:8]
     S4[1] = s4[8:16]
-    gx = copy(S4.at[sib], wgr, ms_s.at[1], ms_r.at[5], at_core)
+    columns = wg_hbm.at[:, pl.ds(pl.multiple_of(c * HALF, HALF), HALF)]
+    gx = copy(S4.at[sib], columns, ms_s.at[1], ms_r.at[5], at_core)
     gx.start()
-
-    settle(W.at[sib], recv=ms_r.at[2], dev=at_core)
-    mean += project(sib)
-    coef = rs * rs * (mean / D)
-    stores = [
-        pltpu.make_async_copy(a, b, out_s.at[i])
-        for i, (a, b) in enumerate(((keys, keys_hbm), (wg, wg_hbm), (gg, gg_hbm)))
-    ]
-    stores[0].start()
+    wg_out = pltpu.make_async_copy(S4.at[c], columns, out_s.at[1])
+    wg_out.start()
 
     def back(k, carry):
         cols = pl.ds(pl.multiple_of(k * WIDE, WIDE), WIDE)
@@ -508,31 +510,10 @@
 
     lax.fori_loop(0, gtiles, back, 0)
 
-    gx.wait_recv()
-    own, other = S4[c], wgr[...]
-    wg[:, 0:HALF] = jnp.where(c == 0, own, other)
-    wg[:, HALF:2 * HALF] = jnp.where(c == 0, other, own)
-    stores[1].start()
-    settle(qxr.at[pl.ds(0, 7)], recv=ms_r.at[7], dev=at_core)
-    same = qx[...] + qxr[1] + qxr[4] + qxr[5]
-    next_x = (qxr[2] + qxr[3]) + (qxr[6] + qxr[7])
-    row = lax.broadcasted_iota(jnp.int32, (2 * Z, Z), 0)
-    zcol = lax.broadcasted_iota(jnp.int32, (2 * Z, Z), 1)
-    total = sum(
-        jnp.dot(
-            jnp.where(row == 2 * zcol + p, 1.0, 0.0), v,
-            precision=lax.Precision.HIGHEST, preferred_element_type=F32,
-        )
-        for p, v in ((xlo, same), (1 - xlo, next_x))
-    )
-    gg[...] = total * inverse / gain[...]
-    stores[2].start()
-
     wx.wait_send()
-    gx.wait_send()
     for ref, i in (
         (G.at[sib], 0), (W.at[c], 3), (S3.at[pl.ds(0, Z - 1)], 4),
-        (qz.at[pl.ds(0, Z - 1)], 5), (qyr.at[pl.ds(0, 3)], 6), (qxr.at[pl.ds(0, 7)], 7),
+        (qz.at[pl.ds(0, Z - 1)], 5), (qyr.at[pl.ds(0, 3)], 6),
     ):
         settle(ref, send=ms_s.at[i], dev=at_core)
 
@@ -548,26 +529,56 @@
     get_x.sent(three)
     get_yx.sent(W.at[c, pl.ds(0, hz), :, pl.ds(0, 3)])
     get_xy.sent(W.at[c, pl.ds(0, hz), :, pl.ds(0, 3)])
+
+    gx.wait_recv()
+    settle(qxr.at[pl.ds(1, 7)], recv=ms_r.at[7], dev=at_core)
+    gx.wait_send()
+    settle(qxr.at[pl.ds(1, 7)], send=ms_s.at[7], dev=at_core)
     pltpu.make_async_copy(tig, tig_hbm, out_s.at[3]).wait()
-    for d in stores:
+    for d in (keys_out, wg_out, qx_out):
         d.wait()
 
 
-def keep(keys, tig, wg, gg, keys_out, tig_out, wg_out, gg_out, keys_v, tig_v, wg_v, gg_v, in_s, out_s):
-    step = tig.shape[0] // 4
-    moves = [(keys, keys_v, keys_out), (wg, wg_v, wg_out), (gg, gg_v, gg_out)]
-    for i in range(4):
+def keep(
+    inverse, keys, tig, wg, qxr, gain, keys_out, tig_out, wg_out, gg_out,
+    keys_v, tig_v, wg_v, qxr_v, gain_v, gg_v, in_s, out_s,
+):
+    loads = [pltpu.make_async_copy(a, v, in_s.at[i]) for i, (a, v) in enumerate(((qxr, qxr_v), (gain, gain_v)))]
+    step = tig.shape[0] // 8
+    moves = []
+    for i in range(8):
         part = pl.ds(i * step, step)
         moves.append((tig.at[part], tig_v.at[part], tig_out.at[part]))
-    reads = [pltpu.make_async_copy(a, v, in_s.at[i]) for i, (a, v, _) in enumerate(moves)]
+    moves += [(keys, keys_v, keys_out), (wg, wg_v, wg_out)]
+    reads = [pltpu.make_async_copy(a, v, in_s.at[2 + i]) for i, (a, v, _) in enumerate(moves)]
     writes = [pltpu.make_async_copy(v, b, out_s.at[i]) for i, (_, v, b) in enumerate(moves)]
-    for d in reads:
+    for d in loads + reads:
         d.start()
-    for r, w in zip(reads, writes):
+    for r, w in zip(reads[:4], writes[:4]):
+        r.wait()
+        w.start()
+    for d in loads:
+        d.wait()
+    Z = qxr_v.shape[1]
+    xlo = lax.axis_index("node") % 2
+    same = qxr_v[0] + qxr_v[1] + qxr_v[4] + qxr_v[5]
+    next_x = (qxr_v[2] + qxr_v[3]) + (qxr_v[6] + qxr_v[7])
+    row = lax.broadcasted_iota(jnp.int32, (2 * Z, 2 * Z), 0)
+    col = lax.broadcasted_iota(jnp.int32, (2 * Z, 2 * Z), 1)
+    order = jnp.where(row == jnp.where(col < Z, 2 * col + xlo, 2 * (col - Z) + 1 - xlo), 1.0, 0.0)
+    total = jnp.dot(
+        order, jnp.concatenate([same, next_x], axis=0),
+        precision=lax.Precision.HIGHEST, preferred_element_type=F32,
+    )
+    gg_v[...] = total * inverse / gain_v[...]
+    gg_write = pltpu.make_async_copy(gg_v, gg_out, out_s.at[len(moves)])
+    gg_write.start()
+    for r, w in zip(reads[4:], writes[4:]):
         r.wait()
         w.start()
     for w in writes:
         w.wait()
+    gg_write.wait()
 
 
 def local(tokens, gain, w_codes, w_scales, seq_counts, key_grad):
@@ -589,12 +600,12 @@
             jax.ShapeDtypeStruct((rows, 2 * HALF), BF16),
             jax.ShapeDtypeStruct((rows, D), BF16),
             jax.ShapeDtypeStruct((8, 2 * HALF), F32),
-            jax.ShapeDtypeStruct((2 * Z, 128), F32),
+            jax.ShapeDtypeStruct((8, Z, 128), F32),
         ),
-        in_specs=[hbm] * 6,
+        in_specs=[pl.BlockSpec(memory_space=pltpu.HBM)] + [hbm] * 5,
         out_specs=(hbm,) * 4,
         scratch_shapes=[
-            pltpu.VMEM((1, 1), jnp.int32),
+            pltpu.SMEM((1,), jnp.int32),
             pltpu.VMEM((rows, D), BF16),
             pltpu.VMEM((rows, 2 * HALF), BF16),
             pltpu.VMEM(w_codes.shape, BF16),
@@ -602,8 +613,6 @@
             pltpu.VMEM((D // 128, 128), F32),
             pltpu.VMEM((rows, 2 * HALF), BF16),
             pltpu.VMEM((rows, D), BF16),
-            pltpu.VMEM((8, 2 * HALF), F32),
-            pltpu.VMEM((2 * Z, 128), F32),
             pltpu.VMEM((2, 8, HALF), F32),
             pltpu.VMEM((2, Z, 2, 4, 2, 16, HALF), BF16),
             pltpu.VMEM((rows, 2 * HALF), BF16),
@@ -621,13 +630,11 @@
             pltpu.VMEM((Z, 16, HALF), BF16),
             pltpu.VMEM((Z, 16, HALF), BF16),
             pltpu.VMEM((2, 8, HALF), F32),
-            pltpu.VMEM((8, HALF), F32),
             pltpu.VMEM((1, Z * 16), F32),
             pltpu.VMEM((Z, 1, Z * 16), F32),
             pltpu.VMEM((Z, 128), F32),
             pltpu.VMEM((4, Z, 128), F32),
             pltpu.VMEM((Z, 128), F32),
-            pltpu.VMEM((8, Z, 128), F32),
             pltpu.SemaphoreType.REGULAR((2,)),
             dma((9,)),
             dma((4,)),
@@ -639,15 +646,17 @@
         compiler_params=pltpu.CompilerParams(
             collective_id=0, has_side_effects=True, vmem_limit_bytes=VMEM_BYTES
         ),
-    )(seq_counts.reshape(1, 1), tokens, key_grad, w_codes, w_scales, gain.reshape(D // 128, 128))
+    )(seq_counts, tokens, key_grad, w_codes, w_scales, gain.reshape(D // 128, 128))
+    gains = jax.ShapeDtypeStruct((D // 128, 128), F32)
+    kept = [jax.ShapeDtypeStruct(o.shape, o.dtype) for o in outs]
     keys, tig, wg, gg = pl.pallas_call(
-        keep,
-        out_shape=tuple(jax.ShapeDtypeStruct(o.shape, o.dtype) for o in outs),
-        in_specs=[hbm] * 4,
+        functools.partial(keep, inverse),
+        out_shape=(*kept[:3], gains),
+        in_specs=[hbm] * 5,
         out_specs=(hbm,) * 4,
-        scratch_shapes=[pltpu.VMEM(o.shape, o.dtype) for o in outs] + [dma((7,)), dma((7,))],
+        scratch_shapes=[pltpu.VMEM(o.shape, o.dtype) for o in (*kept, gains, gains)] + [dma((12,)), dma((11,))],
         compiler_params=pltpu.CompilerParams(vmem_limit_bytes=VMEM_BYTES),
-    )(*outs)
+    )(*outs, gain.reshape(D // 128, 128))
     return keys, tig, wg, gg.reshape(D)
 
 

time: 57.1 us -> 56.5 us (0.989)
  Pallas kernels: 55.6 us -> 55 us
    pallas_call x1, Pallas kernels: 53 us -> 52.4 us  [local(): pl.pallas_call(functools.partial(kernel, Z, inverse), out_shape=(jax.Shap...]
where the time goes in v6:
time: 56.5 us; the launch traced here: 56.3 us
  Pallas kernels  55 us (97%)
  between operations  1.29 us (2%)
    pallas_call x1, Pallas kernels, local(): pl.pallas_call(functools.partial(kernel, Z, inverse), out_shape=(jax.Shap...  52.4 us
    pallas_call x1, Pallas kernels, local(): pl.pallas_call(functools.partial(keep, inverse), out_shape=(*kept[:3], ga...  2.66 us

profile of v6, /device:TPU:1, one launch (start us, length us, event | category | flops | bytes accessed | tf_op | source)
XLA Modules:
  0.0 56.3 jit_solution(920474619858545332)
XLA Ops:
  1.3 52.4 %shard_map.93 = (bf16[256,512]{1,0:T(8,128)(2,1)}, bf16[256,4096]{1,0:T(8,128)(2,1)}, f32[8,512]{1,0:T(8,128)}, f32[8,16,128]{2,1,0:T(8,128)}) custom-call(s32[1]{0:T(128)S(6)} %copy.10.cnt_hbm, bf16[256,4096]{1,0:T(8,128)(2,1)} %tok_hbm.1, bf16[256,512]{1,0:T(8,128)(2,1)} %kg_hbm.1, bf16[4,8,128]{2,1,0:T(8,128)(2,1)} %codes_hbm.1, bf16[4,8]{1,0:T(4,128)(2,1)} %scales_hbm.1, ...), custom_call_target="tpu_custom_call" | custom-call | tf_op jit(solution)/shard_map/pallas_call | solution.py:597
  53.7 2.7 %shard_map.94 = (bf16[256,512]{1,0:T(8,128)(2,1)}, bf16[256,4096]{1,0:T(8,128)(2,1)}, f32[8,512]{1,0:T(8,128)}, f32[32,128]{1,0:T(8,128)}) custom-call(bf16[256,512]{1,0:T(8,128)(2,1)} %get-tuple-element.12.keys, bf16[256,4096]{1,0:T(8,128)(2,1)} %get-tuple-element.13.tig, f32[8,512]{1,0:T(8,128)} %get-tuple-element.14.wg, ...), custom_call_target="tpu_custom_call" | custom-call | tf_op jit(solution)/shard_map/pallas_call | solution.py:652

commit v7 on v6

--- a/solution.py
+++ b/solution.py
@@ -191,8 +191,8 @@
         k = (i + 1) // 2
         return Z // 2 + k - 2 * k * (i % 2)
 
-    def at_y(o):
-        return (node, ((y + o) % 4) * 4 + xhi * 2 + c)
+    def at_y(o, core):
+        return (node, ((y + o) % 4) * 4 + xhi * 2 + core)
 
     def at_x(o, core):
         xx = (x + o) % 4
@@ -331,7 +331,7 @@
     def sems(i, pair, j, n):
         return ms_s.at[i], pair.at[pl.ds(j, n)]
 
-    devs_y = [at_y(o) for o in range(4)]
+    devs_y = [at_y(o, c) for o in range(4)]
     devs_x = [at_x(o, c) for o in range(4)]
     low, high = pl.ds(0, hz), pl.ds(hz, hz)
     sum_y = RingSum(
@@ -376,12 +376,18 @@
     settle(W.at[c, pl.ds(0, Z - 1), xlo, y, xhi], recv=ms_r.at[1], dev=at_core)
     get_y.start()
     get_x.start()
+    def terms(first):
+        part = pl.ds(first, hz)
+        wide, lanes = hz * 16, Z * 16
+        q = jnp.sum(W[c, part, xlo, y, xhi].astype(F32) * S3[part].astype(F32), axis=2, keepdims=True)
+        row = lax.broadcasted_iota(jnp.int32, (wide, lanes), 0) + first * 16
+        diag = row == lax.broadcasted_iota(jnp.int32, (wide, lanes), 1)
+        return jnp.sum(jnp.where(diag, q.reshape(wide, 1), 0.0), axis=0, keepdims=True)
+
     sum_yx.finish(S3, 0)
+    low_terms = terms(0)
     sum_xy.finish(S3, hz)
-
-    q = jnp.sum(W[c, :, xlo, y, xhi].astype(F32) * S3[...].astype(F32), axis=2, keepdims=True).reshape(Z * 16, 1)
-    diag = lax.broadcasted_iota(jnp.int32, (Z * 16, Z * 16), 0) == lax.broadcasted_iota(jnp.int32, (Z * 16, Z * 16), 1)
-    qs[...] = jnp.sum(jnp.where(diag, q, 0.0), axis=0, keepdims=True)
+    qs[...] = low_terms + terms(hz)
 
     def gqz(o, src_z):
         return copy(qs, qz.at[src_z], ms_s.at[5], ms_r.at[4], at_z(o))
@@ -429,16 +435,19 @@
         src = (z + Z - o) % Z
         return acc + qz[src]
 
-    settle(qz.at[pl.ds(0, Z - 1)], recv=ms_r.at[4], dev=at_core)
-    qsum = lax.fori_loop(1, Z, gqz_add, qs[...])
     lane = lax.broadcasted_iota(jnp.int32, (Z, Z * 16), 1)
     zrow = lax.broadcasted_iota(jnp.int32, (Z, Z * 16), 0)
-    spread = jnp.where((lane >= zrow * 16) & (lane < zrow * 16 + 16), qsum, 0.0)
     src = lax.broadcasted_iota(jnp.int32, (Z * 16, 128), 0)
     to = lax.broadcasted_iota(jnp.int32, (Z * 16, 128), 1)
     place = jnp.where((src & 15) + (y * 2 + xhi) * 16 == to, 1.0, 0.0)
+    settle(qz.at[pl.ds(0, Z - 1)], recv=ms_r.at[4], dev=at_core)
+    qsum = lax.fori_loop(1, Z, gqz_add, qs[...])
+    spread = jnp.where((lane >= zrow * 16) & (lane < zrow * 16 + 16), qsum, 0.0)
     qy[...] = jnp.dot(spread, place, precision=lax.Precision.HIGHEST, preferred_element_type=F32)
-    qys = [copy(qy, qyr.at[o], ms_s.at[6], ms_r.at[6], at_y(o)) for o in (1, 2, 3)]
+    qys = [
+        copy(qy, qyr.at[2 * o + r], ms_s.at[6], ms_r.at[6], at_y(o, sib if r else c))
+        for o in range(4) for r in range(2) if o or r
+    ]
     for d in qys:
         d.start()
 
@@ -462,23 +471,6 @@
         return jnp.sum(kf * kg[:, cols].astype(F32), axis=1, keepdims=True)
 
     mean = project(c)
-
-    settle(W.at[sib], recv=ms_r.at[2], dev=at_core)
-    settle(qyr.at[pl.ds(0, 3)], recv=ms_r.at[6], dev=at_core)
-    qx[...] = qy[...] + qyr[1] + qyr[2] + qyr[3]
-    qxs = [
-        copy(qx, qxr.at[2 * o + r], ms_s.at[7], ms_r.at[7], at_x(o, sib if r else c))
-        for o in range(4) for r in range(2) if o or r
-    ]
-    for d in qxs:
-        d.start()
-    qx_out = pltpu.make_async_copy(qx, qxr.at[0], out_s.at[0])
-    qx_out.start()
-
-    mean += project(sib)
-    coef = rs * rs * (mean / D)
-    keys_out = pltpu.make_async_copy(keys, keys_hbm, out_s.at[2])
-    keys_out.start()
 
     def rsz_add(o, acc):
         src = (z + Z - o) % Z
@@ -496,24 +488,38 @@
     wg_out = pltpu.make_async_copy(S4.at[c], columns, out_s.at[1])
     wg_out.start()
 
+    settle(W.at[sib], recv=ms_r.at[2], dev=at_core)
+    mean += project(sib)
+    coef = rs * rs * (mean / D)
+    keys_out = pltpu.make_async_copy(keys, keys_hbm, out_s.at[2])
+    keys_out.start()
+
+    settle(qyr.at[pl.ds(1, 7)], recv=ms_r.at[6], dev=at_core)
+    qx[...] = sum((qyr[i] for i in range(1, 8)), qy[...])
+    qxs = [copy(qx, qxr.at[o], ms_s.at[7], ms_r.at[7], at_x(o, c)) for o in (1, 2, 3)]
+    for d in qxs:
+        d.start()
+    qx_out = pltpu.make_async_copy(qx, qxr.at[0], out_s.at[0])
+    qx_out.start()
+
     def back(k, carry):
-        cols = pl.ds(pl.multiple_of(k * WIDE, WIDE), WIDE)
+        cols = pl.ds(pl.multiple_of(k * span, span), span)
         d = -(tok[:, cols].astype(F32) * coef)
         for h in range(2):
             d += lax.dot_general(
-                M[:, h * HALF:(h + 1) * HALF], W[h, pl.ds(k * gt, gt)].reshape(WIDE, HALF),
+                M[:, h * HALF:(h + 1) * HALF], W[h, pl.ds(k * hz, hz)].reshape(span, HALF),
                 (((1,), (1,)), ((), ())), preferred_element_type=F32,
             )
         tig[:, cols] = d.astype(BF16)
         pltpu.make_async_copy(tig.at[:, cols], tig_hbm.at[:, cols], out_s.at[3]).start()
         return carry
 
-    lax.fori_loop(0, gtiles, back, 0)
+    lax.fori_loop(0, 2, back, 0)
 
     wx.wait_send()
     for ref, i in (
         (G.at[sib], 0), (W.at[c], 3), (S3.at[pl.ds(0, Z - 1)], 4),
-        (qz.at[pl.ds(0, Z - 1)], 5), (qyr.at[pl.ds(0, 3)], 6),
+        (qz.at[pl.ds(0, Z - 1)], 5), (qyr.at[pl.ds(1, 7)], 6),
     ):
         settle(ref, send=ms_s.at[i], dev=at_core)
 
@@ -531,9 +537,9 @@
     get_xy.sent(W.at[c, pl.ds(0, hz), :, pl.ds(0, 3)])
 
     gx.wait_recv()
-    settle(qxr.at[pl.ds(1, 7)], recv=ms_r.at[7], dev=at_core)
+    settle(qxr.at[pl.ds(1, 3)], recv=ms_r.at[7], dev=at_core)
     gx.wait_send()
-    settle(qxr.at[pl.ds(1, 7)], send=ms_s.at[7], dev=at_core)
+    settle(qxr.at[pl.ds(1, 3)], send=ms_s.at[7], dev=at_core)
     pltpu.make_async_copy(tig, tig_hbm, out_s.at[3]).wait()
     for d in (keys_out, wg_out, qx_out):
         d.wait()
@@ -561,8 +567,8 @@
         d.wait()
     Z = qxr_v.shape[1]
     xlo = lax.axis_index("node") % 2
-    same = qxr_v[0] + qxr_v[1] + qxr_v[4] + qxr_v[5]
-    next_x = (qxr_v[2] + qxr_v[3]) + (qxr_v[6] + qxr_v[7])
+    same = qxr_v[0] + qxr_v[2]
+    next_x = qxr_v[1] + qxr_v[3]
     row = lax.broadcasted_iota(jnp.int32, (2 * Z, 2 * Z), 0)
     col = lax.broadcasted_iota(jnp.int32, (2 * Z, 2 * Z), 1)
     order = jnp.where(row == jnp.where(col < Z, 2 * col + xlo, 2 * (col - Z) + 1 - xlo), 1.0, 0.0)
@@ -600,7 +606,7 @@
             jax.ShapeDtypeStruct((rows, 2 * HALF), BF16),
             jax.ShapeDtypeStruct((rows, D), BF16),
             jax.ShapeDtypeStruct((8, 2 * HALF), F32),
-            jax.ShapeDtypeStruct((8, Z, 128), F32),
+            jax.ShapeDtypeStruct((4, Z, 128), F32),
         ),
         in_specs=[pl.BlockSpec(memory_space=pltpu.HBM)] + [hbm] * 5,
         out_specs=(hbm,) * 4,
@@ -633,7 +639,7 @@
             pltpu.VMEM((1, Z * 16), F32),
             pltpu.VMEM((Z, 1, Z * 16), F32),
             pltpu.VMEM((Z, 128), F32),
-            pltpu.VMEM((4, Z, 128), F32),
+            pltpu.VMEM((8, Z, 128), F32),
             pltpu.VMEM((Z, 128), F32),
             pltpu.SemaphoreType.REGULAR((2,)),
             dma((9,)),

time: 56.5 us -> 55.6 us (0.984)
  Pallas kernels: 55 us -> 54.1 us
    pallas_call x1, Pallas kernels: 52.4 us -> 51.5 us  [local(): pl.pallas_call(functools.partial(kernel, Z, inverse), out_shape=(jax.Shap...]
where the time goes in v7:
time: 55.6 us; the launch traced here: 55.4 us
  Pallas kernels  54.1 us (97%)
  between operations  1.29 us (2%)
    pallas_call x1, Pallas kernels, local(): pl.pallas_call(functools.partial(kernel, Z, inverse), out_shape=(jax.Shap...  51.5 us
    pallas_call x1, Pallas kernels, local(): pl.pallas_call(functools.partial(keep, inverse), out_shape=(*kept[:3], ga...  2.64 us

profile of v7, /device:TPU:1, one launch (start us, length us, event | category | flops | bytes accessed | tf_op | source)
XLA Modules:
  0.0 55.4 jit_solution(219922958139116330)
XLA Ops:
  1.3 51.5 %shard_map.93 = (bf16[256,512]{1,0:T(8,128)(2,1)}, bf16[256,4096]{1,0:T(8,128)(2,1)}, f32[8,512]{1,0:T(8,128)}, f32[4,16,128]{2,1,0:T(8,128)}) custom-call(s32[1]{0:T(128)S(6)} %copy.10.cnt_hbm, bf16[256,4096]{1,0:T(8,128)(2,1)} %tok_hbm.1, bf16[256,512]{1,0:T(8,128)(2,1)} %kg_hbm.1, bf16[4,8,128]{2,1,0:T(8,128)(2,1)} %codes_hbm.1, bf16[4,8]{1,0:T(4,128)(2,1)} %scales_hbm.1, ...), custom_call_target="tpu_custom_call" | custom-call | tf_op jit(solution)/shard_map/pallas_call | solution.py:603
  52.7 2.6 %shard_map.94 = (bf16[256,512]{1,0:T(8,128)(2,1)}, bf16[256,4096]{1,0:T(8,128)(2,1)}, f32[8,512]{1,0:T(8,128)}, f32[32,128]{1,0:T(8,128)}) custom-call(bf16[256,512]{1,0:T(8,128)(2,1)} %get-tuple-element.12.keys, bf16[256,4096]{1,0:T(8,128)(2,1)} %get-tuple-element.13.tig, f32[8,512]{1,0:T(8,128)} %get-tuple-element.14.wg, ...), custom_call_target="tpu_custom_call" | custom-call | tf_op jit(solution)/shard_map/pallas_call | solution.py:658

commit v8 on v7

--- a/solution.py
+++ b/solution.py
@@ -51,9 +51,13 @@
         self.r0 = one(2, 3, near, self.lr.at[1, near], minus)
         self.r1 = one(2, 3, far, self.lr.at[1, far], minus)
 
-    def start(self):
-        for d in (self.to_a, self.to_b, self.l1, self.r0):
-            d.start()
+    def start_near(self):
+        self.to_a.start()
+        self.r0.start()
+
+    def start_far(self):
+        self.to_b.start()
+        self.l1.start()
 
     def add(self, o, base, buf):
         def body(k, carry):
@@ -361,10 +365,14 @@
         block = W.at[c, part, :, ys[o]]
         copy(block, block, ms_s.at[3], ms_r.at[2], at_core).start()
 
-    lax.fori_loop(0, gtiles // 2, core_add, 0)
-    sum_y.start()
-    lax.fori_loop(gtiles // 2, gtiles, core_add, 0)
-    sum_x.start()
+    core_add(0, 0)
+    sum_y.start_near()
+    core_add(1, 0)
+    sum_y.start_far()
+    core_add(2, 0)
+    sum_x.start_near()
+    core_add(3, 0)
+    sum_x.start_far()
 
     sum_y.forward()
     sum_x.forward()

time: 55.6 us -> 55.4 us (level)
  no operation moved by 1% of the time
where the time goes in v8:
time: 55.4 us; the launch traced here: 55.2 us
  Pallas kernels  53.9 us (97%)
  between operations  1.29 us (2%)
    pallas_call x1, Pallas kernels, local(): pl.pallas_call(functools.partial(kernel, Z, inverse), out_shape=(jax.Shap...  51.3 us
    pallas_call x1, Pallas kernels, local(): pl.pallas_call(functools.partial(keep, inverse), out_shape=(*kept[:3], ga...  2.64 us

profile of v8, /device:TPU:1, one launch (start us, length us, event | category | flops | bytes accessed | tf_op | source)
XLA Modules:
  0.0 55.2 jit_solution(2462776642129483990)
XLA Ops:
  1.3 51.3 %shard_map.93 = (bf16[256,512]{1,0:T(8,128)(2,1)}, bf16[256,4096]{1,0:T(8,128)(2,1)}, f32[8,512]{1,0:T(8,128)}, f32[4,16,128]{2,1,0:T(8,128)}) custom-call(s32[1]{0:T(128)S(6)} %copy.10.cnt_hbm, bf16[256,4096]{1,0:T(8,128)(2,1)} %tok_hbm.1, bf16[256,512]{1,0:T(8,128)(2,1)} %kg_hbm.1, bf16[4,8,128]{2,1,0:T(8,128)(2,1)} %codes_hbm.1, bf16[4,8]{1,0:T(4,128)(2,1)} %scales_hbm.1, ...), custom_call_target="tpu_custom_call" | custom-call | tf_op jit(solution)/shard_map/pallas_call | solution.py:611
  52.6 2.6 %shard_map.94 = (bf16[256,512]{1,0:T(8,128)(2,1)}, bf16[256,4096]{1,0:T(8,128)(2,1)}, f32[8,512]{1,0:T(8,128)}, f32[32,128]{1,0:T(8,128)}) custom-call(bf16[256,512]{1,0:T(8,128)(2,1)} %get-tuple-element.12.keys, bf16[256,4096]{1,0:T(8,128)(2,1)} %get-tuple-element.13.tig, f32[8,512]{1,0:T(8,128)} %get-tuple-element.14.wg, ...), custom_call_target="tpu_custom_call" | custom-call | tf_op jit(solution)/shard_map/pallas_call | solution.py:666
